TPU v7x, 256 devices: a whole 4x4x8 slice. The times are simulated.
256 devices in a mesh: gx: 16 (over y, x_lo, core), gy: 16 (over z, x_hi).
Axes of the slice: x: 4 (x_hi: 2, x_lo: 2; x = x_hi * 2 + x_lo), y: 4, z: 8, core: 2. Of those that a mesh axis runs over, the one named last changes fastest.
Arguments:
- tokens: bfloat16 [131072, 6144], P(('gx', 'gy')), may hold values from -24 to 24
- cotangent: bfloat16 [131072, 6144], P(('gx', 'gy')), may hold values from -0.0625 to 0.0625
- weights: float32 [6144, 512], P(('gx', 'gy')), may hold values from -1 to 1
- first_moment: float32 [6144, 512], P(('gx', 'gy')), may hold values from -0.012 to 0.012
- second_moment: float32 [6144, 512], P(('gx', 'gy')), may hold values from 1e-06 to 0.0001
- norm_gain: float32 [6144], P(('gx', 'gy')), may hold values from 0.5 to 1.5
- gain_first: float32 [6144], P(('gx', 'gy')), may hold values from -3 to 3
- gain_second: float32 [6144], P(('gx', 'gy')), may hold values from 0.05 to 5
Outputs:
- new_weights: float32 [6144, 512], P(('gx', 'gy'))
- new_first: float32 [6144, 512], P(('gx', 'gy'))
- new_second: float32 [6144, 512], P(('gx', 'gy'))
- new_gain: float32 [6144], P(('gx', 'gy'))
- new_gain_first: float32 [6144], P(('gx', 'gy'))
- new_gain_second: float32 [6144], P(('gx', 'gy'))
- next_weights: bfloat16 [6144, 512], replicated
- next_gain: bfloat16 [6144], replicated
All inputs are finite; a program needn't handle non-finite values.
Results may differ from a plain program's by a relative error of at most 0.007.
The roundings to bfloat16 on the way count: a program that leaves them out, or rounds other values in their place, can miss the bound.
Values may be sent and summed in bfloat16 or wider, within the bound.
A program may use at most 128 MiB of HBM per device.

v0:
```python
import jax
import jax.numpy as jnp
from jax import lax
from jax.sharding import PartitionSpec as P

IMG_TOK = 256


EPS_NORM = 1e-06
BETA_ONE = 0.9
BETA_TWO = 0.95
LEARN_RATE = 0.001
DECAY_RATE = 0.1
ADAM_EPS = 1e-08
CORRECT_ONE = 1.0 - 0.9**10
CORRECT_TWO = 1.0 - 0.95**10


def normalize(values):
    average = jnp.mean(values, axis=-1, keepdims=True)
    centred = values - average
    inverse = lax.rsqrt(jnp.mean(centred * centred, axis=-1, keepdims=True) + EPS_NORM)
    return (centred * inverse, inverse)


def norm_back(grad_hat, normed, inverse):
    first_part = jnp.mean(grad_hat, axis=-1, keepdims=True)
    second_part = normed * jnp.mean(grad_hat * normed, axis=-1, keepdims=True)
    return inverse * (grad_hat - first_part - second_part)


def product(form, left, right):
    return jnp.einsum(form, left, right, preferred_element_type=jnp.float32)


def local_terms(tokens, cotangent, low_weights, low_gain):
    total_rows, features = tokens.shape
    count_img = total_rows // IMG_TOK
    head_dim = low_weights.shape[1] // 4
    standard, ignored = normalize(tokens.astype(jnp.float32))
    normed = (standard * low_gain.astype(jnp.float32)).astype(jnp.bfloat16)
    projected = jnp.dot(normed, low_weights[:, : 3 * head_dim], preferred_element_type=jnp.float32)
    query_hat, query_inverse = normalize(projected[:, :head_dim])
    key_hat, key_inverse = normalize(projected[:, head_dim : 2 * head_dim])
    query_low = query_hat.astype(jnp.bfloat16).reshape(count_img, IMG_TOK, head_dim)
    key_low = key_hat.astype(jnp.bfloat16).reshape(count_img, IMG_TOK, head_dim)
    value_low = (
        projected[:, 2 * head_dim :].astype(jnp.bfloat16).reshape(count_img, IMG_TOK, head_dim)
    )
    scaling = head_dim ** (-0.5)
    scores = product("nsh,nth->nst", query_low, key_low) * scaling
    exponent = jnp.exp(scores)
    attention = exponent / jnp.sum(exponent, axis=-1, keepdims=True)
    attention_low = attention.astype(jnp.bfloat16)
    attended = product("nst,nth->nsh", attention_low, value_low).astype(jnp.bfloat16)
    attended = attended.reshape(total_rows, head_dim)
    grad_out = lax.dot_general(
        cotangent, attended, (((0,), (0,)), ((), ())), preferred_element_type=jnp.float32
    )
    grad_attended = jnp.dot(
        cotangent, low_weights[:, 3 * head_dim :], preferred_element_type=jnp.float32
    )
    grad_attended = grad_attended.astype(jnp.bfloat16).reshape(count_img, IMG_TOK, head_dim)
    grad_value = product("nst,nsh->nth", attention_low, grad_attended).astype(jnp.bfloat16)
    grad_attention = product("nsh,nth->nst", grad_attended, value_low)
    row_total = jnp.sum(attention * grad_attention, axis=-1, keepdims=True)
    grad_scores = (attention * (grad_attention - row_total) * scaling).astype(jnp.bfloat16)
    grad_query_hat = product("nst,nth->nsh", grad_scores, key_low).reshape(total_rows, head_dim)
    grad_key_hat = product("nst,nsh->nth", grad_scores, query_low).reshape(total_rows, head_dim)
    grad_query = norm_back(grad_query_hat, query_hat, query_inverse).astype(jnp.bfloat16)
    grad_key = norm_back(grad_key_hat, key_hat, key_inverse).astype(jnp.bfloat16)
    grad_proj = jnp.concatenate(
        [grad_query, grad_key, grad_value.reshape(total_rows, head_dim)], axis=1
    )
    grad_in = lax.dot_general(
        normed, grad_proj, (((0,), (0,)), ((), ())), preferred_element_type=jnp.float32
    )
    grad_normed = lax.dot_general(
        grad_proj,
        low_weights[:, : 3 * head_dim],
        (((1,), (1,)), ((), ())),
        preferred_element_type=jnp.float32,
    )
    grad_gain = jnp.sum(grad_normed * standard, axis=0)
    return (jnp.concatenate([grad_in, grad_out], axis=1), grad_gain)


def adam_step(parameter, moment_one, moment_two, gradient, decay_rate):
    fresh_one = BETA_ONE * moment_one + (1.0 - BETA_ONE) * gradient
    fresh_two = BETA_TWO * moment_two + (1.0 - BETA_TWO) * gradient * gradient
    adjusted = fresh_one / CORRECT_ONE / (jnp.sqrt(fresh_two / CORRECT_TWO) + ADAM_EPS)
    return (parameter - LEARN_RATE * (adjusted + decay_rate * parameter), fresh_one, fresh_two)


def shards(
    tokens, cotangent, weights, first_moment, second_moment, norm_gain, gain_first, gain_second
):
    low_weights = weights.astype(jnp.bfloat16)
    low_gain = norm_gain.astype(jnp.bfloat16)
    group_pair = (
        lax.all_gather(low_weights, "gy", axis=0, tiled=True),
        lax.all_gather(low_gain, "gy", axis=0, tiled=True),
    )
    full_weights, full_gain = (
        lax.all_gather(group_pair[0], "gx", axis=0, tiled=True),
        lax.all_gather(group_pair[1], "gx", axis=0, tiled=True),
    )
    term_weights, term_gain = local_terms(tokens, cotangent, full_weights, full_gain)
    group_sums = (
        lax.psum_scatter(term_weights, "gx", scatter_dimension=0, tiled=True),
        lax.psum_scatter(term_gain, "gx", scatter_dimension=0, tiled=True),
    )
    grad_weights, grad_gain = (
        lax.psum_scatter(group_sums[0], "gy", scatter_dimension=0, tiled=True),
        lax.psum_scatter(group_sums[1], "gy", scatter_dimension=0, tiled=True),
    )
    new_weights, new_first, new_second = adam_step(
        weights, first_moment, second_moment, grad_weights, DECAY_RATE
    )
    new_gain, new_gain_first, new_gain_second = adam_step(
        norm_gain, gain_first, gain_second, grad_gain, 0.0
    )
    send_weights = new_weights.astype(jnp.bfloat16)
    send_gain = new_gain.astype(jnp.bfloat16)
    group_back = (
        lax.all_gather(send_weights, "gy", axis=0, tiled=True),
        lax.all_gather(send_gain, "gy", axis=0, tiled=True),
    )
    next_weights, next_gain = (
        lax.all_gather(group_back[0], "gx", axis=0, tiled=True),
        lax.all_gather(group_back[1], "gx", axis=0, tiled=True),
    )
    return (
        new_weights,
        new_first,
        new_second,
        new_gain,
        new_gain_first,
        new_gain_second,
        next_weights,
        next_gain,
    )


def solution(mesh):
    in_specs = (
        P(("gx", "gy"), None),
        P(("gx", "gy"), None),
        P(("gx", "gy"), None),
        P(("gx", "gy"), None),
        P(("gx", "gy"), None),
        P(("gx", "gy")),
        P(("gx", "gy")),
        P(("gx", "gy")),
    )
    out_specs = (
        P(("gx", "gy"), None),
        P(("gx", "gy"), None),
        P(("gx", "gy"), None),
        P(("gx", "gy")),
        P(("gx", "gy")),
        P(("gx", "gy")),
        P(),
        P(),
    )
    return jax.shard_map(shards, mesh=mesh, in_specs=in_specs, out_specs=out_specs, check_vma=False)
```

profile of v0, /device:TPU:1, one launch (start us, length us, event | category | flops | bytes accessed | tf_op | source)
XLA Modules:
  0.0 710.0 jit_solution(1096303512400687690)
XLA Ops:
  7.2 0.0 all-gather.5.cloned.1.call-start
  7.2 0.8 convert_element_type.53
  8.0 42.3 %all_gather.26 = bf16[384,512]{1,0:T(8,128)(2,1)} all-gather(bf16[24,512]{1,0:T(8,128)(2,1)S(1)} %convert_element_type.53), channel_id=1, replica_groups=mesh['gx'=16,'gy'=16] {'gy'}, dimensions={0}, use_global_device_ids=true | all-gather | bytes 417792 | tf_op jit(solution)/shard_map/all_gather | solution.py:101
  50.3 0.0 all-gather.5.cloned.1.call-update
  50.4 0.0 reduce-scatter.5.cloned.1.call-start
  50.4 0.7 convert_element_type.50
  51.1 1.3 fusion.63
  53.1 0.2 dynamic-update-slice
  53.3 30.2 %all-reduce = bf16[384]{0:T(512)(128)(2,1)S(1)} all-reduce(bf16[384]{0:T(512)(128)(2,1)S(1)} %dynamic-update-slice), channel_id=1, replica_groups=mesh['gx'=16,'gy'=16] {'gy'}, use_global_device_ids=true, to_apply=%add | all-reduce | flops 384 | bytes 1536
  83.6 33.6 %all-gather = bf16[16,1,384]{2,1,0:T(2,128)(2,1)S(1)} all-gather(bf16[1,1,384]{2,1,0:T(2,128)(2,1)S(1)} %reshape.121), channel_id=1, replica_groups=mesh['gx'=16,'gy'=16] {'gx'}, dimensions={0}, use_global_device_ids=true | all-gather | bytes 13056 | tf_op jit(solution)/shard_map/all_gather | solution.py:106
  117.2 3.7 convert_reduce_fusion
  120.9 0.0 copy-done
  120.9 1.8 fusion.7
  122.7 0.0 all-gather.5.cloned.1.call-done
  122.7 7.3 %fusion.9 = f32[512,384]{1,0:T(8,128)S(1)} fusion(bf16[6144,512]{1,0:T(8,128)(2,1)} %all-gather.5.cloned.1.call-done, bf16[512,6144]{1,0:T(8,128)(2,1)} %param.8, f32[6144]{0:T(1024)S(1)} %bitcast.69, f32[512]{0:T(512)S(1)} %add_rsqrt_fusion.2, f32[512]{0:T(512)S(1)} %broadcast_multiply_fusion.4), kind=kOutput, calls=%fused_computation.13 | convolution fusion | flops 2431647744 | bytes 11825152 | tf_op jit(solution)/shard_map/dot_general | solution.py:42
  130.0 0.2 slice_reduce_fusion
  130.3 0.4 multiply_reduce_fusion.1
  130.7 0.3 fusion.41
  131.0 0.3 fusion.36
  131.3 0.2 fusion.13
  131.6 5.0 fusion.18
  136.6 0.3 convolution_convert_fusion.1
  136.9 0.3 convolution_convert_fusion
  137.2 0.2 fusion.70
  137.4 0.5 fusion.64
  137.9 0.4 fusion.67
  138.3 0.0 slice-start
  138.3 0.5 fusion.34
  138.8 0.0 slice-start.1
  138.9 4.1 convolution_bitcast_fusion
  143.0 0.6 fusion.33
  143.6 0.0 slice-done
  143.6 0.0 slice-done.1
  143.6 3.5 fusion.43
  147.1 4.9 pad_maximum_fusion
  151.9 0.0 reduce-scatter.5.cloned.1.call-update
  152.0 0.0 reduce-scatter.7.cloned.1.call-start
  152.0 136.7 %reduce-scatter.5.cloned.1.call-done = f32[384,512]{0,1:T(8,128)} async-done(((f32[6144,512]{0,1:T(8,128)}), f32[384,512]{0,1:T(8,128)}) %reduce-scatter.5.cloned.1.call-update) | async-done | bytes 786448 | tf_op jit(solution)/shard_map/reduce_scatter | solution.py:110
  288.8 2.3 copy.53
  291.0 0.0 reduce-scatter.7.cloned.1.call-update
  291.1 0.0 all-gather.7.cloned.1.call-start
  291.1 199.4 %reduce-scatter.7.cloned.1.call-done = f32[24,512]{1,0:T(8,128)} async-done(((f32[384,512]{1,0:T(8,128)}), f32[24,512]{1,0:T(8,128)}) %reduce-scatter.7.cloned.1.call-update) | async-done | bytes 49168 | tf_op jit(solution)/shard_map/reduce_scatter | solution.py:114
  490.5 0.0 copy-done.1
  490.5 0.0 copy-done.2
  490.5 0.0 copy-done.3
  490.5 1.5 fusion.61
  492.0 35.7 %all_gather.28 = bf16[384,512]{1,0:T(8,128)(2,1)} all-gather(bf16[24,512]{1,0:T(8,128)(2,1)S(1)} %get-tuple-element.42), channel_id=1, replica_groups=mesh['gx'=16,'gy'=16] {'gy'}, dimensions={0}, use_global_device_ids=true | all-gather | bytes 417792 | tf_op jit(solution)/shard_map/all_gather | solution.py:126
  527.7 0.0 all-gather.7.cloned.1.call-update
  527.7 0.0 copy-done.7
  527.7 0.6 dynamic-slice.2
  529.6 0.0 copy-start.4
  529.6 0.0 copy-start.5
  529.7 0.0 copy-start.6
  529.7 7.3 %fusion.6 = f32[6144]{0:T(1024)S(1)} fusion(bf16[512,6144]{1,0:T(8,128)(2,1)} %param.8, f32[512]{0:T(512)S(1)} %add_rsqrt_fusion.2, f32[512]{0:T(512)S(1)} %broadcast_multiply_fusion.4, bf16[6144,512]{1,0:T(8,128)(2,1)} %all-gather.5.cloned.1.call-done, bf16[512,128]{1,0:T(8,128)(2,1)S(1)} %bitcast.74, bf16[512,128]{1,0:T(8,128)(2,1)S(1)} %get-tuple-element.47, ...), kind=kOutput, calls=%fused_computation.8 | convolution fusion | flops 2432821248 | bytes 11431936 | tf_op jit(solution)/shard_map/dot_general | solution.py:78
  536.9 62.1 %all-reduce.2 = f32[6144]{0:T(1024)S(1)} all-reduce(f32[6144]{0:T(1024)S(1)} %fusion.6), channel_id=4, replica_groups=mesh['gx'=16,'gy'=16] {'gx'}, use_global_device_ids=true, to_apply=%region_15.0.clone | all-reduce | flops 6144 | bytes 49152
  599.0 0.1 dynamic-slice.3
  599.1 30.2 %all-reduce.3 = f32[384]{0:T(512)S(1)} all-reduce(f32[384]{0:T(512)S(1)} %dynamic-slice.3), channel_id=5, replica_groups=mesh['gx'=16,'gy'=16] {'gy'}, use_global_device_ids=true, to_apply=%region_16.0.clone | all-reduce | flops 384 | bytes 3072
  629.3 0.6 fusion.59
  629.9 0.2 dynamic-update-slice.1
  630.1 32.4 %all-reduce.1 = bf16[384]{0:T(512)(128)(2,1)S(1)} all-reduce(bf16[384]{0:T(512)(128)(2,1)S(1)} %dynamic-update-slice.1), channel_id=1, replica_groups=mesh['gx'=16,'gy'=16] {'gy'}, use_global_device_ids=true, to_apply=%add.1 | all-reduce | flops 384 | bytes 1536
  662.5 34.4 %all-gather.1 = bf16[16,1,384]{2,1,0:T(2,128)(2,1)S(1)} all-gather(bf16[1,1,384]{2,1,0:T(2,128)(2,1)S(1)} %reshape.123), channel_id=1, replica_groups=mesh['gx'=16,'gy'=16] {'gx'}, dimensions={0}, use_global_device_ids=true | all-gather | bytes 13056 | tf_op jit(solution)/shard_map/all_gather | solution.py:131
  696.9 0.1 reduce.2
  697.0 0.6 reshape.124
  697.6 5.9 copy.60
  (27 shorter events, 0.1 us)
Async XLA Ops:
  7.2 115.5 %all-gather.5.cloned.1.call-start = ((), (), s32[]{:S(2)}) async-start(), calls=%async_computation.2 | async-start | bytes 6684672 | tf_op jit(solution)/shard_map/all_gather | solution.py:105
  50.4 238.4 %reduce-scatter.5.cloned.1.call-start = ((), (), s32[]{:S(2)}) async-start(), calls=%async_computation.3 | async-start | bytes 13369344 | tf_op jit(solution)/shard_map/reduce_scatter | solution.py:110
  83.5 37.3 %copy-start = (bf16[512,6144]{1,0:T(8,128)(2,1)S(1)}, bf16[512,6144]{1,0:T(8,128)(2,1)}, u32[]{:S(2)}) copy-start(bf16[512,6144]{1,0:T(8,128)(2,1)} %param.8) | copy-start | bytes 18874372
  138.3 5.3 slice-start
  138.8 4.7 slice-start.1
  151.9 338.6 %copy-start.1 = (f32[24,512]{1,0:T(8,128)S(1)}, f32[24,512]{1,0:T(8,128)}, u32[]{:S(2)}) copy-start(f32[24,512]{1,0:T(8,128)} %param.10) | copy-start | bytes 147460
  151.9 338.6 %copy-start.2 = (f32[24,512]{1,0:T(8,128)S(1)}, f32[24,512]{1,0:T(8,128)}, u32[]{:S(2)}) copy-start(f32[24,512]{1,0:T(8,128)} %param.11) | copy-start | bytes 147460
  151.9 338.6 %copy-start.3 = (f32[24,512]{1,0:T(8,128)S(1)}, f32[24,512]{1,0:T(8,128)}, u32[]{:S(2)}) copy-start(f32[24,512]{1,0:T(8,128)} %param.12) | copy-start | bytes 147460
  151.9 375.8 %copy-start.7 = (u32[256]{0:T(256)S(1)}, u32[256]{0:T(256)}, u32[]{:S(2)}) copy-start(u32[256]{0:T(256)} %constant.69) | copy-start | bytes 3076
  152.0 338.6 %reduce-scatter.7.cloned.1.call-start = ((), (), s32[]{:S(2)}) async-start(), calls=%async_computation.5 | async-start | bytes 835584 | tf_op jit(solution)/shard_map/reduce_scatter | solution.py:114
  291.1 406.5 %all-gather.7.cloned.1.call-start = ((), (), s32[]{:S(2)}) async-start(), calls=%async_computation.4 | async-start | bytes 6684672 | tf_op jit(solution)/shard_map/all_gather | solution.py:130
  529.6 99.7 %copy-start.4 = (f32[24]{0:T(128)S(1)}, f32[24]{0:T(128)}, u32[]{:S(2)}) copy-start(f32[24]{0:T(128)} %param.13) | copy-start | bytes 292
  529.6 99.7 %copy-start.5 = (f32[24]{0:T(128)S(1)}, f32[24]{0:T(128)}, u32[]{:S(2)}) copy-start(f32[24]{0:T(128)} %param.14) | copy-start | bytes 292
  529.7 99.7 %copy-start.6 = (f32[24]{0:T(128)S(1)}, f32[24]{0:T(128)}, u32[]{:S(2)}) copy-start(f32[24]{0:T(128)} %param.15) | copy-start | bytes 292
Sparse Core Ops, SparseCore 0:
  50.5 48.5 all-gather.4
  152.1 136.6 reduce-scatter.4
  293.2 197.3 reduce-scatter.6
  527.9 56.2 all-gather.6
where the time goes:
time: 711 us; the launch traced here: 710 us
  waiting for transfers between devices  336 us (47%)
  blocking collectives  301 us (42%)
  matrix products  29.3 us (4%)
  other arithmetic  16.1 us (2%)
  between operations  16 us (2%)
  local copies, waits for them, and re-layouts  11.3 us (2%)
    reduce_scatter x1, waiting for transfers between devices, shards(): lax.psum_scatter(group_sums[0], 'gy', scatter_dimension=0, tiled=True)  199 us
    unnamed x4, blocking collectives  155 us
    reduce_scatter x1, waiting for transfers between devices, shards(): lax.psum_scatter(term_weights, 'gx', scatter_dimension=0, tiled=True)  137 us
    all_gather x1, blocking collectives, shards(): lax.all_gather(low_weights, 'gy', axis=0, tiled=True)  42.3 us
    all_gather x1, blocking collectives, shards(): lax.all_gather(send_weights, 'gy', axis=0, tiled=True)  35.7 us
    all_gather x1, blocking collectives, shards(): lax.all_gather(group_back[1], 'gx', axis=0, tiled=True)  34.4 us
    all_gather x1, blocking collectives, shards(): lax.all_gather(group_pair[1], 'gx', axis=0, tiled=True)  33.6 us
  transfers between devices with their start and end apart: 4, of which 2 were waited for; matrix products, arithmetic and copies ran while one was open for 2% of the time, Pallas kernels for 0%

commit v1 on v0

--- a/solution.py
+++ b/solution.py
@@ -1,11 +1,13 @@
+import functools
+
 import jax
 import jax.numpy as jnp
 from jax import lax
+from jax.experimental import pallas as pl
+from jax.experimental.pallas import tpu as pltpu
 from jax.sharding import PartitionSpec as P
 
 IMG_TOK = 256
-
-
 EPS_NORM = 1e-06
 BETA_ONE = 0.9
 BETA_TWO = 0.95
@@ -14,6 +16,289 @@
 ADAM_EPS = 1e-08
 CORRECT_ONE = 1.0 - 0.9**10
 CORRECT_TWO = 1.0 - 0.95**10
+MESH = pl.DeviceIdType.MESH
+BF16, F32 = jnp.bfloat16, jnp.float32
+
+VIEW = (2, 2, 2, 2, 4, 2, 48, 512)
+GVIEW = (2, 2, 2, 2, 4, 2, 2, 1, 128)
+FAR = [(dy, dz, dx) for dy in range(2) for dz in range(4) for dx in range(2)][1:]
+ORDERS = (("z", "y", "x"), ("x", "z", "y"), ("y", "x", "z"))
+
+
+class Place:
+    def __init__(self):
+        gx, gy = lax.axis_index("gx"), lax.axis_index("gy")
+        self.y, self.z = gx // 4, gy // 2
+        self.xl, self.c, self.xh = lax.rem(gx // 2, 2), lax.rem(gx, 2), lax.rem(gy, 2)
+        self.yh, self.yl, self.zf, self.zl = self.y // 2, lax.rem(self.y, 2), self.z // 2, lax.rem(self.z, 2)
+        self.x = self.xh * 2 + self.xl
+        self.low = {"x": self.xl, "y": self.yl, "z": self.zl}
+
+    def device(self, x, y, z, c):
+        return (y * 4 + lax.rem(x, 2) * 2 + c, z * 2 + x // 2)
+
+    def step(self, axis, by):
+        x, y, z = self.x, self.y, self.z
+        if axis == "x":
+            x = lax.rem(x + by + 4, 4)
+        elif axis == "y":
+            y = lax.rem(y + by + 4, 4)
+        else:
+            z = lax.rem(z + by + 8, 8)
+        return self.device(x, y, z, self.c)
+
+    def sibling(self):
+        return self.device(self.x, self.y, self.z, 1 - self.c)
+
+    def far(self, offset):
+        dy, dz, dx = offset
+        yh, zf, xh = lax.rem(self.yh + dy, 2), lax.rem(self.zf + dz, 4), lax.rem(self.xh + dx, 2)
+        return yh, zf, xh, self.device(xh * 2 + self.xl, yh * 2 + self.yl, zf * 2 + self.zl, self.c)
+
+
+def enter(me):
+    barrier = pltpu.get_barrier_semaphore()
+    others = [me.far(f)[3] for f in FAR] + [me.step(a, b) for a in "xyz" for b in (1, -1)] + [me.sibling()]
+    for other in others:
+        pl.semaphore_signal(barrier, inc=1, device_id=other, device_id_type=MESH)
+    pl.semaphore_wait(barrier, len(others))
+
+
+def gather_kernel(shard, gain, full, gfull, land, fs, fr, gs, gr, ns, nr, ss, sr):
+    me = Place()
+    enter(me)
+    own = (me.yh * 4 + me.zf) * 2 + me.xh
+    gplace = gfull.at[me.yh, me.yl, me.xl, me.c, me.zf, me.zl, me.xh]
+    gplace[...] = gain[...]
+    sends = []
+
+    def push(src, dst, ssem, rsem, to):
+        copy = pltpu.make_async_remote_copy(src, dst, ssem, rsem, device_id=to, device_id_type=MESH)
+        copy.start()
+        sends.append(copy)
+        return copy
+
+    far = []
+    for k, f in enumerate(FAR):
+        to = me.far(f)[3]
+        far.append(push(shard, land.at[own], fs.at[k], fr.at[k], to))
+        far.append(push(gplace, gplace, gs.at[k], gr.at[k], to))
+    land[own] = shard[...]
+    for copy in far:
+        copy.wait_recv()
+    for yh in range(2):
+        for zf in range(4):
+            a, b = (land[(yh * 4 + zf) * 2 + xh].astype(F32) for xh in range(2))
+            block = jnp.concatenate(
+                [jnp.concatenate([a[:24], b[:24]], 0), jnp.concatenate([a[24:], b[24:]], 0)], 1
+            )
+            full[yh, me.yl, me.xl, me.c, zf, me.zl] = block.astype(BF16)
+
+    def part(ref, done, half, p):
+        at = {a: (slice(None) if a in done else me.low[a]) for a in "xyz"}
+        rows = slice(None) if p is None else pl.ds(16 * p, 16)
+        return ref.at[half, at["y"], at["x"], me.c, :, at["z"], rows]
+
+    def fresh(ref, done, axis, half, p):
+        at = {a: (slice(None) if a in done else me.low[a]) for a in "xyz"}
+        at[axis] = 1 - me.low[axis]
+        rows = slice(None) if p is None else pl.ds(16 * p, 16)
+        return ref.at[half, at["y"], at["x"], me.c, :, at["z"], rows]
+
+    shared = []
+    count = [0]
+
+    def share(ref):
+        k = count[0]
+        count[0] += 1
+        shared.append(push(ref, ref, ss.at[k], sr.at[k], me.sibling()))
+
+    def near(stage, p):
+        order = ORDERS[p]
+        axis, done = order[stage], order[:stage]
+        k = (stage * 3 + p) * 2
+        copies = []
+        for half in range(2):
+            src = part(full, done, half, p)
+            copies.append(push(src, src, ns.at[k + half], nr.at[k + half], me.step(axis, 1 - 2 * half)))
+        return copies
+
+    def near_gain(stage):
+        axis, done = "zyx"[stage], "zyx"[:stage]
+        at = {a: (slice(None) if a in done else me.low[a]) for a in "xyz"}
+        src = gfull.at[:, at["y"], at["x"], me.c, :, at["z"]]
+        return push(src, src, ns.at[18 + stage], nr.at[18 + stage], me.step(axis, 1))
+
+    flight = [near(0, p) for p in range(3)]
+    gflight = near_gain(0)
+    share(full.at[:, me.yl, me.xl, me.c, :, me.zl])
+    for stage in range(3):
+        later = []
+        for p in range(3):
+            for copy in flight[p]:
+                copy.wait_recv()
+            if stage < 2:
+                later.append(near(stage + 1, p))
+            for half in range(2):
+                share(fresh(full, ORDERS[p][:stage], ORDERS[p][stage], half, p))
+        gflight.wait_recv()
+        if stage < 2:
+            gflight = near_gain(stage + 1)
+        flight = later
+    share(gfull.at[:, :, :, me.c])
+    for copy in shared:
+        copy.wait_recv()
+    for copy in sends:
+        copy.wait_send()
+
+
+def gather_all(low_rows, low_gain, ident):
+    shard = jnp.concatenate([low_rows[:, :256], low_rows[:, 256:]], axis=0)
+    gain = jnp.pad(low_gain.astype(F32), (0, 104)).reshape(1, 128)
+    dma = pltpu.SemaphoreType.DMA
+    full, gfull = pl.pallas_call(
+        gather_kernel,
+        name="gather%d" % ident,
+        out_shape=(jax.ShapeDtypeStruct(VIEW, BF16), jax.ShapeDtypeStruct(GVIEW, F32)),
+        in_specs=[pl.BlockSpec(memory_space=pltpu.VMEM)] * 2,
+        out_specs=(pl.BlockSpec(memory_space=pltpu.VMEM),) * 2,
+        scratch_shapes=[
+            pltpu.VMEM((16, 48, 256), BF16),
+            dma((15,)), dma((15,)), dma((15,)), dma((15,)),
+            dma((21,)), dma((21,)), dma((20,)), dma((20,)),
+        ],
+        compiler_params=pltpu.CompilerParams(
+            collective_id=ident, has_side_effects=True, vmem_limit_bytes=40 << 20
+        ),
+    )(shard, gain)
+    return full.reshape(6144, 512), gfull.reshape(256, 128)[:, :24].reshape(6144).astype(BF16)
+
+
+def scatter_kernel(grad, out, acc, sib_out, sib_in, nout, nin, fout, fin, bs, br, ns, nr, fs, fr, load):
+    me = Place()
+    big = pltpu.make_async_copy(grad, acc, load)
+    big.start()
+    enter(me)
+    big.wait()
+    sends = []
+
+    def push(src, dst, ssem, rsem, to):
+        copy = pltpu.make_async_remote_copy(src, dst, ssem, rsem, device_id=to, device_id_type=MESH)
+        copy.start()
+        sends.append(copy)
+        return copy
+
+    sib = []
+    for yh in range(2):
+        for yl in range(2):
+            k = yh * 2 + yl
+
+            def cast(i, carry):
+                xl, zf = i // 4, lax.rem(i, 4)
+                sib_out[yh, yl, xl, zf] = acc[yh, yl, xl, 1 - me.c, zf].astype(BF16)
+                return carry
+
+            lax.fori_loop(0, 8, cast, 0)
+            sib.append(push(sib_out.at[yh, yl], sib_in.at[yh, yl], bs.at[k], br.at[k], me.sibling()))
+    for yh in range(2):
+        for yl in range(2):
+            sib[yh * 2 + yl].wait_recv()
+
+            def add(i, carry):
+                xl, zf = i // 4, lax.rem(i, 4)
+                acc[yh, yl, xl, me.c, zf] += sib_in[yh, yl, xl, zf].astype(F32)
+                return carry
+
+            lax.fori_loop(0, 8, add, 0)
+
+    def combos(stage, p):
+        order = ORDERS[p][::-1]
+        axis, rest, gone = order[stage], order[stage + 1:], order[:stage]
+        found = []
+        for n in range(2 ** len(rest)):
+            found.append({a: (n >> i) & 1 for i, a in enumerate(rest)} | {a: me.low[a] for a in gone})
+        return axis, found
+
+    def base(stage):
+        return (0, 4, 6)[stage]
+
+    def near(stage, p):
+        axis, found = combos(stage, p)
+        copies = []
+        for half in range(2):
+            for n, at in enumerate(found):
+                yl, xl, zl = ((1 - me.low[a]) if a == axis else at[a] for a in "yxz")
+                nout[p, half, base(stage) + n] = acc[
+                    half, yl, xl, me.c, :, zl, pl.ds(16 * p, 16), :
+                ].astype(BF16)
+            where = (p, half, pl.ds(base(stage), len(found)))
+            k = (stage * 3 + p) * 2 + half
+            copies.append(push(nout.at[where], nin.at[where], ns.at[k], nr.at[k], me.step(axis, 1 - 2 * half)))
+        return copies
+
+    def near_add(stage, p, copies):
+        axis, found = combos(stage, p)
+        for half in range(2):
+            copies[half].wait_recv()
+            for n, at in enumerate(found):
+                yl, xl, zl = (me.low[a] if a == axis else at[a] for a in "yxz")
+                place = (half, yl, xl, me.c, slice(None), zl, pl.ds(16 * p, 16), slice(None))
+                acc[place] = acc[place] + nin[p, half, base(stage) + n].astype(F32)
+
+    flight = [near(0, p) for p in range(3)]
+    for stage in range(3):
+        later = []
+        for p in range(3):
+            near_add(stage, p, flight[p])
+            if stage < 2:
+                later.append(near(stage + 1, p))
+        flight = later
+
+    def mine(yh, zf, xh):
+        block = acc[yh, me.yl, me.xl, me.c, zf, me.zl]
+        return block[:24] if xh == 0 else block[24:]
+
+    for yh in range(2):
+        for zf in range(4):
+            for xh in range(2):
+                rows = mine(yh, zf, xh)
+                fout[(yh * 4 + zf) * 2 + xh] = jnp.concatenate([rows[:, :256], rows[:, 256:]], 0)
+    fcopies = []
+    for k, f in enumerate(FAR):
+        yh, zf, xh, to = me.far(f)
+        fcopies.append(push(fout.at[(yh * 4 + zf) * 2 + xh], fin.at[k], fs.at[k], fr.at[k], to))
+    total = fout[(me.yh * 4 + me.zf) * 2 + me.xh]
+    for k in range(15):
+        fcopies[k].wait_recv()
+        total = total + fin[k]
+    out[:, :256] = total[:24]
+    out[:, 256:] = total[24:]
+    for copy in sends:
+        copy.wait_send()
+
+
+def scatter_sum(grad, ident):
+    dma = pltpu.SemaphoreType.DMA
+    return pl.pallas_call(
+        scatter_kernel,
+        name="scatter%d" % ident,
+        out_shape=jax.ShapeDtypeStruct((24, 512), F32),
+        in_specs=[pl.BlockSpec(memory_space=pl.ANY)],
+        out_specs=pl.BlockSpec(memory_space=pltpu.VMEM),
+        scratch_shapes=[
+            pltpu.VMEM((2, 2, 2, 2, 4, 2, 48, 512), F32),
+            pltpu.VMEM((2, 2, 2, 4, 2, 48, 512), BF16),
+            pltpu.VMEM((2, 2, 2, 4, 2, 48, 512), BF16),
+            pltpu.VMEM((3, 2, 7, 4, 16, 512), BF16),
+            pltpu.VMEM((3, 2, 7, 4, 16, 512), BF16),
+            pltpu.VMEM((16, 48, 256), F32),
+            pltpu.VMEM((15, 48, 256), F32),
+            dma((4,)), dma((4,)), dma((18,)), dma((18,)), dma((15,)), dma((15,)), dma(()),
+        ],
+        compiler_params=pltpu.CompilerParams(
+            collective_id=ident, has_side_effects=True, vmem_limit_bytes=48 << 20
+        ),
+    )(grad.reshape(VIEW))
 
 
 def normalize(values):
@@ -75,14 +360,7 @@
     grad_in = lax.dot_general(
         normed, grad_proj, (((0,), (0,)), ((), ())), preferred_element_type=jnp.float32
     )
-    grad_normed = lax.dot_general(
-        grad_proj,
-        low_weights[:, : 3 * head_dim],
-        (((1,), (1,)), ((), ())),
-        preferred_element_type=jnp.float32,
-    )
-    grad_gain = jnp.sum(grad_normed * standard, axis=0)
-    return (jnp.concatenate([grad_in, grad_out], axis=1), grad_gain)
+    return jnp.concatenate([grad_in, grad_out], axis=1)
 
 
 def adam_step(parameter, moment_one, moment_two, gradient, decay_rate):
@@ -97,38 +375,20 @@
 ):
     low_weights = weights.astype(jnp.bfloat16)
     low_gain = norm_gain.astype(jnp.bfloat16)
-    group_pair = (
-        lax.all_gather(low_weights, "gy", axis=0, tiled=True),
-        lax.all_gather(low_gain, "gy", axis=0, tiled=True),
-    )
-    full_weights, full_gain = (
-        lax.all_gather(group_pair[0], "gx", axis=0, tiled=True),
-        lax.all_gather(group_pair[1], "gx", axis=0, tiled=True),
-    )
-    term_weights, term_gain = local_terms(tokens, cotangent, full_weights, full_gain)
-    group_sums = (
-        lax.psum_scatter(term_weights, "gx", scatter_dimension=0, tiled=True),
-        lax.psum_scatter(term_gain, "gx", scatter_dimension=0, tiled=True),
-    )
-    grad_weights, grad_gain = (
-        lax.psum_scatter(group_sums[0], "gy", scatter_dimension=0, tiled=True),
-        lax.psum_scatter(group_sums[1], "gy", scatter_dimension=0, tiled=True),
-    )
+    full_weights, full_gain = gather_all(low_weights, low_gain, 1)
+    terms = local_terms(tokens, cotangent, full_weights, full_gain)
+    grad_weights = scatter_sum(terms, 2)
+    grad_gain = jnp.sum(
+        grad_weights[:, :384] * low_weights[:, :384].astype(F32), axis=1
+    ) / low_gain.astype(F32)
     new_weights, new_first, new_second = adam_step(
         weights, first_moment, second_moment, grad_weights, DECAY_RATE
     )
     new_gain, new_gain_first, new_gain_second = adam_step(
         norm_gain, gain_first, gain_second, grad_gain, 0.0
     )
-    send_weights = new_weights.astype(jnp.bfloat16)
-    send_gain = new_gain.astype(jnp.bfloat16)
-    group_back = (
-        lax.all_gather(send_weights, "gy", axis=0, tiled=True),
-        lax.all_gather(send_gain, "gy", axis=0, tiled=True),
-    )
-    next_weights, next_gain = (
-        lax.all_gather(group_back[0], "gx", axis=0, tiled=True),
-        lax.all_gather(group_back[1], "gx", axis=0, tiled=True),
+    next_weights, next_gain = gather_all(
+        new_weights.astype(jnp.bfloat16), new_gain.astype(jnp.bfloat16), 3
     )
     return (
         new_weights,
@@ -143,24 +403,11 @@
 
 
 def solution(mesh):
-    in_specs = (
-        P(("gx", "gy"), None),
-        P(("gx", "gy"), None),
-        P(("gx", "gy"), None),
-        P(("gx", "gy"), None),
-        P(("gx", "gy"), None),
-        P(("gx", "gy")),
-        P(("gx", "gy")),
-        P(("gx", "gy")),
-    )
-    out_specs = (
-        P(("gx", "gy"), None),
-        P(("gx", "gy"), None),
-        P(("gx", "gy"), None),
-        P(("gx", "gy")),
-        P(("gx", "gy")),
-        P(("gx", "gy")),
-        P(),
-        P(),
-    )
-    return jax.shard_map(shards, mesh=mesh, in_specs=in_specs, out_specs=out_specs, check_vma=False)
+    rows, line = P(("gx", "gy"), None), P(("gx", "gy"))
+    return jax.shard_map(
+        shards,
+        mesh=mesh,
+        in_specs=(rows,) * 5 + (line,) * 3,
+        out_specs=(rows,) * 3 + (line,) * 3 + (P(), P()),
+        check_vma=False,
+    )

time: 711 us -> 199 us (0.28)
  waiting for transfers between devices: 336 us -> 0 us
  blocking collectives: 301 us -> 0 us
  Pallas kernels: 0 us -> 136 us
  between operations: 16 us -> 1 us
  local copies, waits for them, and re-layouts: 11.3 us -> 25 us
  matrix products: 29.3 us -> 21.4 us
    reduce_scatter x2 -> x0, waiting for transfers between devices: 336 us -> none  [the longest x1 199 us: shards(): lax.psum_scatter(group_sums[0], 'gy', scatter_dimension=0, tiled=True)]
    unnamed x4 -> x0, blocking collectives: 155 us -> none
    all_gather x4 -> x0, blocking collectives: 146 us -> none  [the longest x1 42.3 us: shards(): lax.all_gather(low_weights, 'gy', axis=0, tiled=True)]
    pallas_call x0 -> x3, Pallas kernels: none -> 136 us  [the longest x2 86 us: gather_all(): pl.pallas_call(gather_kernel, name='gather%d' % ident, out_shape=(jax.Sha...]
    concatenate x0 -> x1, local copies, waits for them, and re-layouts: none -> 12.6 us  [local_terms(): return jnp.concatenate([grad_in, grad_out], axis=1)]
    dot_general x1 -> x0, matrix products: 7.25 us -> none  [local_terms(): lax.dot_general(grad_proj, low_weights[:, :3 * head_dim], (((1,), (1,)),...]
  transfers between devices with their start and end apart: 4 -> 0, of which waited for: 2 -> 0; matrix products, arithmetic and copies ran while one was open for 2% -> 0% of each run, Pallas kernels for 0% -> 0%
where the time goes in v1:
time: 199 us
  Pallas kernels  136 us (68%)
  local copies, waits for them, and re-layouts  25 us (13%)
  matrix products  21.4 us (11%)
  other arithmetic  15.1 us (8%)
    pallas_call x2, Pallas kernels, gather_all(): pl.pallas_call(gather_kernel, name='gather%d' % ident, out_shape=(jax.Sha...  86 us
    pallas_call x1, Pallas kernels, scatter_sum(): pl.pallas_call(scatter_kernel, name='scatter%d' % ident, out_shape=jax.Sh...  50.4 us
    concatenate x1, local copies, waits for them, and re-layouts, local_terms(): return jnp.concatenate([grad_in, grad_out], axis=1)  12.6 us
    unnamed x29, local copies, waits for them, and re-layouts  11.4 us
    dot_general x1, matrix products, local_terms(): jnp.dot(normed, low_weights[:, :3 * head_dim], preferred_element_type=jnp...  5.92 us
    dot_general x1, matrix products, local_terms(): jnp.dot(cotangent, low_weights[:, 3 * head_dim:], preferred_element_type=...  5.65 us
    concatenate x1, other arithmetic, local_terms(): return jnp.concatenate([grad_in, grad_out], axis=1)  4.86 us
    reduce_sum x2, other arithmetic, normalize(): average = jnp.mean(values, axis=-1, keepdims=True)  4.28 us

profile of v1, /device:TPU:1, one launch (start us, length us, event | category | flops | bytes accessed | tf_op | source)
XLA Modules:
  0.0 199.0 jit_solution(15355470158975462776)
XLA Ops:
  0.6 0.0 copy-start.3
  0.6 0.8 convert_convert_fusion
  1.5 0.0 copy-start.4
  1.5 4.1 %convert_reduce_fusion = f32[512]{0:T(512)S(1)} fusion(bf16[512,6144]{1,0:T(8,128)(2,1)} %param.8), kind=kLoop, calls=%fused_computation.2 | loop fusion | flops 6290944 | bytes 6293504 | tf_op jit(solution)/shard_map/reduce_sum | solution.py:305
  5.5 0.0 copy-done.3
  5.5 1.8 fusion.3
  7.3 0.0 copy-done.4
  7.4 46.6 %gather1.1 = (bf16[2,2,2,2,4,2,48,512]{7,6,5,4,3,2,1,0:T(8,128)(2,1)S(1)}, f32[2,2,2,2,4,2,2,1,128]{8,7,6,5,4,3,2,1,0:T(1,128)S(1)}) custom-call(bf16[48,256]{1,0:T(8,128)(2,1)S(1)} %pad_maximum_fusion.1.shard, f32[1,128]{1,0:T(1,128)S(1)} %pad_bitcast_fusion.gain), custom_call_target="tpu_custom_call" | custom-call | tf_op jit(solution)/shard_map/gather1/pallas_call | solution.py:159
  53.9 0.0 copy-start.1
  54.0 2.7 %copy-done.1 = bf16[2,2,2,2,4,2,48,512]{7,6,5,4,3,2,1,0:T(8,128)(2,1)} copy-done((bf16[2,2,2,2,4,2,48,512]{7,6,5,4,3,2,1,0:T(8,128)(2,1)}, bf16[2,2,2,2,4,2,48,512]{7,6,5,4,3,2,1,0:T(8,128)(2,1)S(1)}, u32[]{:S(2)}) %copy-start.1) | copy-done | bytes 6291480
  56.7 0.1 convert.15
  56.8 0.1 reshape.159
  56.9 0.0 copy-start.2
  57.0 5.6 %fusion.18 = bf16[512,128]{0,1:T(8,128)(2,1)S(1)} fusion(bf16[512,6144]{1,0:T(8,128)(2,1)} %param.9, bf16[6144,512]{1,0:T(8,128)(2,1)} %bitcast.65), kind=kOutput, calls=%fused_computation.23 | convolution fusion | flops 805371904 | bytes 7995392 | tf_op jit(solution)/shard_map/dot_general | solution.py:345
  62.6 0.0 copy-done.2
  62.6 5.9 %fusion.6 = f32[512,384]{1,0:T(8,128)S(1)} fusion(bf16[6144,512]{1,0:T(8,128)(2,1)S(1)} %bitcast.66, bf16[512,6144]{1,0:T(8,128)(2,1)} %param.8, f32[6144]{0:T(1024)S(1)} %reshape.159, f32[512]{0:T(512)S(1)} %add_rsqrt_fusion.2, f32[512]{0:T(512)S(1)} %broadcast_multiply_fusion.4), kind=kOutput, calls=%fused_computation.10 | convolution fusion | flops 2431647744 | bytes 11825152 | tf_op jit(solution)/shard_map/dot_general | solution.py:327
  68.5 0.1 copy.28
  68.7 0.2 slice_reduce_fusion
  68.9 0.4 multiply_reduce_fusion.1
  69.3 0.3 fusion.47
  69.7 0.3 fusion.42
  70.0 0.2 fusion.10
  70.2 0.3 convolution_convert_fusion.1
  70.5 0.3 convolution_convert_fusion
  70.8 0.2 fusion.76
  71.0 0.5 fusion.70
  71.5 0.4 fusion.73
  72.0 0.5 fusion.40
  72.5 0.0 slice-start
  72.5 0.6 fusion.39
  73.1 0.0 slice-start.1
  73.1 4.1 %convolution_bitcast_fusion = f32[6144,128]{0,1:T(8,128)S(1)} fusion(bf16[512,128]{1,0:T(8,128)(2,1)S(1)} %bitcast.80, bf16[512,6144]{1,0:T(8,128)(2,1)} %param.9), kind=kOutput, calls=%fused_computation.9 | convolution fusion | flops 805306368 | bytes 9568256 | tf_op jit(solution)/shard_map/dot_general | solution.py:342
  77.3 0.0 slice-done
  77.3 0.0 slice-done.1
  77.3 3.5 %fusion.27 = f32[6144,384]{0,1:T(8,128)S(1)} fusion(bf16[512,128]{1,0:T(8,128)(2,1)S(1)} %bitcast.85, bf16[512,128]{1,0:T(8,128)(2,1)S(1)} %get-tuple-element.31, bf16[512,128]{1,0:T(8,128)(2,1)S(1)} %get-tuple-element.30, bf16[512,6144]{1,0:T(8,128)(2,1)S(1)} %bitcast.69, f32[6144]{0:T(1024)S(1)} %reshape.159, f32[512]{0:T(512)S(1)} %add_rsqrt_fusion.2, ...), kind=kOutput, calls=%fused_computation.29 | convolution fusion | flops 2432827392 | bytes 16150528 | tf_op jit(solution)/shard_map/dot_general | solution.py:360
  80.8 4.9 %pad_maximum_fusion = f32[6144,512]{0,1:T(8,128)} fusion(f32[6144,128]{0,1:T(8,128)S(1)} %convolution_bitcast_fusion, f32[6144,384]{0,1:T(8,128)S(1)} %fusion.27), kind=kLoop, calls=%fused_computation.8 | loop fusion | flops 3145728 | bytes 25165824 | tf_op jit(solution)/shard_map/concatenate | solution.py:363
  85.7 12.6 %copy.25 = f32[6144,512]{1,0:T(8,128)} copy(f32[6144,512]{0,1:T(8,128)} %pad_maximum_fusion) | data formatting | bytes 25165824 | tf_op jit(solution)/shard_map/concatenate | solution.py:363
  98.3 0.0 copy-start.7
  98.3 0.0 copy-start.8
  98.3 0.0 copy-start.9
  98.3 0.0 copy-start.5
  98.3 0.0 copy-start.6
  98.3 50.4 %scatter2.1 = f32[24,512]{1,0:T(8,128)S(1)} custom-call(f32[2,2,2,2,4,2,48,512]{7,6,5,4,3,2,1,0:T(8,128)} %bitcast.67), custom_call_target="tpu_custom_call" | custom-call | tf_op jit(solution)/shard_map/scatter2/pallas_call | solution.py:282
  148.7 0.1 multiply_reduce_fusion.3
  148.8 0.0 copy-done.7
  148.8 0.0 copy-done.8
  148.8 0.0 copy-done.9
  148.8 0.5 fusion.64
  149.4 0.0 copy-done.5
  149.4 0.0 copy-done.6
  149.4 0.7 fusion.66
  150.1 39.5 %gather3.1 = (bf16[2,2,2,2,4,2,48,512]{7,6,5,4,3,2,1,0:T(8,128)(2,1)S(1)}, f32[2,2,2,2,4,2,2,1,128]{8,7,6,5,4,3,2,1,0:T(1,128)S(1)}) custom-call(bf16[48,256]{1,0:T(8,128)(2,1)S(1)} %pad_maximum_fusion.2.shard, f32[1,128]{1,0:T(1,128)S(1)} %bitcast_convert_fusion.gain), custom_call_target="tpu_custom_call" | custom-call | tf_op jit(solution)/shard_map/gather3/pallas_call | solution.py:159
  189.6 0.0 copy-start
  189.6 2.7 %copy-done = bf16[2,2,2,2,4,2,48,512]{7,6,5,4,3,2,1,0:T(8,128)(2,1)} copy-done((bf16[2,2,2,2,4,2,48,512]{7,6,5,4,3,2,1,0:T(8,128)(2,1)}, bf16[2,2,2,2,4,2,48,512]{7,6,5,4,3,2,1,0:T(8,128)(2,1)S(1)}, u32[]{:S(2)}) %copy-start) | copy-done | bytes 6291480
  192.2 0.1 convert.17
  192.4 0.7 convert_element_type.100
  193.1 5.9 %copy.34 = bf16[6144,512]{1,0:T(8,128)(2,1)} copy(bf16[6144,512]{1,0:T(8,128)(2,1)} %bitcast.64) | data formatting | bytes 12582912
  (23 shorter events, 0.2 us)
Async XLA Ops:
  0.6 4.9 %copy-start.3 = (bf16[512,6144]{1,0:T(8,128)(2,1)S(1)}, bf16[512,6144]{1,0:T(8,128)(2,1)}, u32[]{:S(2)}) copy-start(bf16[512,6144]{1,0:T(8,128)(2,1)} %param.8) | copy-start | bytes 18874372
  1.5 5.9 %copy-start.4 = (f32[24,512]{1,0:T(8,128)S(1)}, f32[24,512]{1,0:T(8,128)}, u32[]{:S(2)}) copy-start(f32[24,512]{1,0:T(8,128)} %param.10) | copy-start | bytes 147460
  53.9 2.7 %copy-start.1 = (bf16[2,2,2,2,4,2,48,512]{7,6,5,4,3,2,1,0:T(8,128)(2,1)}, bf16[2,2,2,2,4,2,48,512]{7,6,5,4,3,2,1,0:T(8,128)(2,1)S(1)}, u32[]{:S(2)}) copy-start(bf16[2,2,2,2,4,2,48,512]{7,6,5,4,3,2,1,0:T(8,128)(2,1)S(1)} %get-tuple-element.13) | copy-start | bytes 18874372
  56.9 5.7 %copy-start.2 = (bf16[2,2,2,2,4,2,48,512]{7,6,5,4,3,2,1,0:T(8,128)(2,1)S(1)}, bf16[2,2,2,2,4,2,48,512]{7,6,5,4,3,2,1,0:T(8,128)(2,1)}, u32[]{:S(2)}) copy-start(bf16[2,2,2,2,4,2,48,512]{7,6,5,4,3,2,1,0:T(8,128)(2,1)} %copy-done.1) | copy-start | bytes 18874372
  72.5 4.8 %slice-start = ((s8[6291456]{0:T(1024)(128)(4,1)}), s8[4194304]{0:T(1024)(128)(4,1)S(1)}, s32[]{:S(2)}) async-start(s8[6291456]{0:T(1024)(128)(4,1)} %bitcast.68), calls=%async_computation | async-start | bytes 8388608
  73.1 4.2 %slice-start.1 = ((s8[6291456]{0:T(1024)(128)(4,1)}), s8[2097152]{0:T(1024)(128)(4,1)S(1)}, s32[]{:S(2)}) async-start(s8[6291456]{0:T(1024)(128)(4,1)} %bitcast.68), calls=%async_computation.1 | async-start | bytes 4194304
  98.3 50.6 %copy-start.7 = (f32[24]{0:T(128)S(1)}, f32[24]{0:T(128)}, u32[]{:S(2)}) copy-start(f32[24]{0:T(128)} %param.13) | copy-start | bytes 292
  98.3 50.6 %copy-start.8 = (f32[24]{0:T(128)S(1)}, f32[24]{0:T(128)}, u32[]{:S(2)}) copy-start(f32[24]{0:T(128)} %param.14) | copy-start | bytes 292
  98.3 50.6 %copy-start.9 = (f32[24]{0:T(128)S(1)}, f32[24]{0:T(128)}, u32[]{:S(2)}) copy-start(f32[24]{0:T(128)} %param.15) | copy-start | bytes 292
  98.3 51.1 %copy-start.5 = (f32[24,512]{1,0:T(8,128)S(1)}, f32[24,512]{1,0:T(8,128)}, u32[]{:S(2)}) copy-start(f32[24,512]{1,0:T(8,128)} %param.11) | copy-start | bytes 147460
  98.3 51.1 %copy-start.6 = (f32[24,512]{1,0:T(8,128)S(1)}, f32[24,512]{1,0:T(8,128)}, u32[]{:S(2)}) copy-start(f32[24,512]{1,0:T(8,128)} %param.12) | copy-start | bytes 147460
  189.6 2.7 %copy-start = (bf16[2,2,2,2,4,2,48,512]{7,6,5,4,3,2,1,0:T(8,128)(2,1)}, bf16[2,2,2,2,4,2,48,512]{7,6,5,4,3,2,1,0:T(8,128)(2,1)S(1)}, u32[]{:S(2)}) copy-start(bf16[2,2,2,2,4,2,48,512]{7,6,5,4,3,2,1,0:T(8,128)(2,1)S(1)} %get-tuple-element.14) | copy-start | bytes 18874372

commit v2 on v0

v2 whole, which is shorter than its diff:
```python
import functools

import jax
import jax.numpy as jnp
from jax import lax
from jax.experimental import pallas as pl
from jax.experimental.pallas import tpu as pltpu
from jax.sharding import PartitionSpec as P

IMG_TOK = 256
EPS_NORM = 1e-06
BETA_ONE = 0.9
BETA_TWO = 0.95
LEARN_RATE = 0.001
DECAY_RATE = 0.1
ADAM_EPS = 1e-08
CORRECT_ONE = 1.0 - 0.9**10
CORRECT_TWO = 1.0 - 0.95**10
MESH = pl.DeviceIdType.MESH
BF16, F32 = jnp.bfloat16, jnp.float32

VIEW = (2, 2, 2, 2, 4, 2, 48, 512)
GVIEW = (2, 2, 2, 2, 4, 2, 2, 1, 128)
ROWS, HEAD, CHUNK = 512, 128, 384
FAR_Z = [(0, dz, 0) for dz in (1, 3, 2)]
FAR_XY = [(0, 0, 1), (1, 0, 0), (1, 0, 1)]
EARLY, LATE = pl.ds(0, 32), pl.ds(32, 16)
ORDERS = (("z", "y", "x"), ("x", "z", "y"), ("y", "x", "z"))


class Place:
    def __init__(self):
        gx, gy = lax.axis_index("gx"), lax.axis_index("gy")
        self.y, self.z = gx // 4, gy // 2
        self.xl, self.c, self.xh = lax.rem(gx // 2, 2), lax.rem(gx, 2), lax.rem(gy, 2)
        self.yh, self.yl, self.zf, self.zl = self.y // 2, lax.rem(self.y, 2), self.z // 2, lax.rem(self.z, 2)
        self.x = self.xh * 2 + self.xl
        self.low = {"x": self.xl, "y": self.yl, "z": self.zl}

    def device(self, x, y, z, c):
        return (y * 4 + lax.rem(x, 2) * 2 + c, z * 2 + x // 2)

    def step(self, axis, by):
        x, y, z = self.x, self.y, self.z
        if axis == "x":
            x = lax.rem(x + by + 4, 4)
        elif axis == "y":
            y = lax.rem(y + by + 4, 4)
        else:
            z = lax.rem(z + by + 8, 8)
        return self.device(x, y, z, self.c)

    def sibling(self):
        return self.device(self.x, self.y, self.z, 1 - self.c)

    def far(self, offset):
        dy, dz, dx = offset
        yh, zf, xh = lax.rem(self.yh + dy, 2), lax.rem(self.zf + dz, 4), lax.rem(self.xh + dx, 2)
        return yh, zf, xh, self.device(xh * 2 + self.xl, yh * 2 + self.yl, zf * 2 + self.zl, self.c)


def enter(me):
    barrier = pltpu.get_barrier_semaphore()
    others = [me.far(f)[3] for f in FAR_Z + FAR_XY] + [me.step(a, b) for a in "xyz" for b in (1, -1)] + [me.sibling()]
    for other in others:
        pl.semaphore_signal(barrier, inc=1, device_id=other, device_id_type=MESH)
    pl.semaphore_wait(barrier, len(others))


class Mail:
    def __init__(self):
        self.sends = []

    def push(self, src, dst, ssem, rsem, to):
        copy = pltpu.make_async_remote_copy(src, dst, ssem, rsem, device_id=to, device_id_type=MESH)
        copy.start()
        self.sends.append(copy)
        return copy

    def close(self):
        for copy in self.sends:
            copy.wait_send()


def gather(me, mail, shard, full, gfull, land, sems, between, result=None, rsem=None):
    fs, fr, gs, gr, ns, nr, ss, sr = sems
    yh, zf, xh = me.yh, me.zf, me.xh
    land[yh, zf, xh] = shard[...]

    def far(first, src_z, src_xy):
        copies = []
        for group, src in ((FAR_Z, src_z), (FAR_XY, src_xy)):
            for f in group:
                k = first + len(copies)
                copies.append(mail.push(src, src, fs.at[k], fr.at[k], me.far(f)[3]))
        return copies

    def far_gain(first, group, src):
        return [
            mail.push(src, src, gs.at[first + k], gr.at[first + k], me.far(f)[3]) for k, f in enumerate(group)
        ]

    own_gain = gfull.at[:, me.yl, me.xl, me.c, :, me.zl]
    gains = far_gain(0, FAR_Z, own_gain.at[yh, zf, xh])
    copies = far(0, land.at[yh, zf, xh, EARLY], land.at[yh, zf, xh, LATE])
    between[0]()
    for copy in gains:
        copy.wait_recv()
    gains = far_gain(3, FAR_XY, own_gain.at[yh, :, xh])
    for copy in copies:
        copy.wait_recv()
    copies = far(6, land.at[:, zf, :, LATE], land.at[yh, :, xh, EARLY])
    between[1]()
    for copy in gains + copies:
        copy.wait_recv()

    def near_gain(stage):
        axis, done = "zyx"[stage], "zyx"[:stage]
        at = {a: (slice(None) if a in done else me.low[a]) for a in "xyz"}
        src = gfull.at[:, at["y"], at["x"], me.c, :, at["z"]]
        return mail.push(src, src, gs.at[6 + stage], gr.at[6 + stage], me.step(axis, 1))

    gflight = near_gain(0)
    for h in range(2):
        for f in range(4):
            a, b = (land[h, f, g].astype(F32) for g in range(2))
            block = jnp.concatenate(
                [jnp.concatenate([a[:24], b[:24]], 0), jnp.concatenate([a[24:], b[24:]], 0)], 1
            )
            full[h, me.yl, me.xl, me.c, f, me.zl] = block.astype(BF16)

    def part(ref, done, half, zfar, p, fresh=None):
        at = {a: (slice(None) if a in done else me.low[a]) for a in "xyz"}
        if fresh is not None:
            at[fresh] = 1 - me.low[fresh]
        return ref.at[half, at["y"], at["x"], me.c, zfar, at["z"], pl.ds(16 * p, 16)]

    shared, local = [], []

    def share(view, src):
        k = len(shared)
        to = src if result is None else result
        shared.append(mail.push(view(src), view(to), ss.at[k], sr.at[k], me.sibling()))
        if result is not None:
            local.append(pltpu.make_async_copy(view(src), view(result), rsem.at[k]))
            local[-1].start()

    both = slice(None)
    flight = {}

    def near(stage, q):
        for p in range(3):
            axis, done = ORDERS[p][stage], ORDERS[p][:stage]
            for half in range(2):
                if stage > 0:
                    flight[stage - 1, p, half, q].wait_recv()
                src = part(full, done, half, pl.ds(2 * q, 2), p)
                k = ((stage * 3 + p) * 2 + half) * 2 + q
                flight[stage, p, half, q] = mail.push(src, src, ns.at[k], nr.at[k], me.step(axis, 1 - 2 * half))

    def spread_news(stage, zfar):
        for p in range(3):
            share(lambda ref: part(ref, ORDERS[p][:stage], both, zfar, p, ORDERS[p][stage]), full)

    near(0, 0)
    near(0, 1)
    share(lambda ref: ref.at[:, me.yl, me.xl, me.c, :, me.zl], full)
    between[2]()
    for stage in (1, 2):
        gflight.wait_recv()
        gflight = near_gain(stage)
        near(stage, 0)
        near(stage, 1)
        spread_news(stage - 1, both)
        between[2 + stage]()
    gflight.wait_recv()
    place = gfull.at[:, :, :, me.c]
    shared.append(mail.push(place, place, ss.at[7], sr.at[7], me.sibling()))
    between[5](shared[-1])
    for q in range(2):
        for p in range(3):
            for half in range(2):
                flight[2, p, half, q].wait_recv()
        spread_news(2, pl.ds(2 * q, 2))
    between[6]()
    for k, copy in enumerate(shared):
        if k != 7:
            copy.wait_recv()
    for copy in local:
        copy.wait()


def gain_rows(gfull):
    feature = lax.broadcasted_iota(jnp.int32, (128, CHUNK), 1).astype(F32)
    lane = lax.broadcasted_iota(jnp.int32, (128, CHUNK), 0).astype(F32)
    spread = jnp.where(feature - 24.0 * jnp.floor((feature + 0.5) * (1.0 / 24.0)) == lane, 1.0, 0.0).astype(BF16)
    feature = lax.broadcasted_iota(jnp.int32, (16, CHUNK), 1)
    source = lax.broadcasted_iota(jnp.int32, (16, CHUNK), 0)
    pick = jnp.where((feature >= 24 * source) & (feature < 24 * source + 24), 1.0, 0.0)
    flat = gfull[...].reshape(256, 128).astype(BF16)
    wide = jnp.dot(flat, spread, preferred_element_type=F32)
    return jnp.sum(wide.reshape(16, 16, CHUNK) * pick[None], axis=1)


def columns(j):
    return pl.ds(pl.multiple_of(j * CHUNK, 128), CHUNK)


def statistics(tok, mean, inverse, first, count):
    def rows(i, carry):
        at = pl.ds(pl.multiple_of(i * 16, 16), 16)
        values = tok[at, :].astype(F32)
        average = jnp.mean(values, axis=-1, keepdims=True)
        centred = values - average
        spread = jnp.mean(centred * centred, axis=-1, keepdims=True)
        mean[at, :] = average
        inverse[at, :] = lax.rsqrt(spread + EPS_NORM)
        return carry

    lax.fori_loop(first, first + count, rows, 0)


def scale_tokens(tok, gains, mean, inverse, c):
    def chunk(i, carry):
        j = i * 2 + c
        at = columns(j)
        standard = (tok[:, at].astype(F32) - mean[...]) * inverse[...]
        tok[:, at] = (standard * gains[pl.ds(j, 1), :]).astype(BF16)
        return carry

    lax.fori_loop(0, 8, chunk, 0)


def project(tok, cot, full, proj, c, first):
    at = [columns(i * 2 + c) for i in range(8)]
    low = full[:, :, :, c].reshape(8 * CHUNK, 4 * HEAD)
    inner = jnp.dot(jnp.concatenate([tok[:, a] for a in at], 1), low[:, : 3 * HEAD], preferred_element_type=F32)
    outer = jnp.dot(jnp.concatenate([cot[:, a] for a in at], 1), low[:, 3 * HEAD :], preferred_element_type=F32)
    if not first:
        inner, outer = inner + proj[:, : 3 * HEAD], outer + proj[:, 3 * HEAD :]
    proj[:, : 3 * HEAD] = inner
    proj[:, 3 * HEAD :] = outer


def normalize(values):
    average = jnp.mean(values, axis=-1, keepdims=True)
    centred = values - average
    inverse = lax.rsqrt(jnp.mean(centred * centred, axis=-1, keepdims=True) + EPS_NORM)
    return (centred * inverse, inverse)


def norm_back(grad_hat, normed, inverse):
    first_part = jnp.mean(grad_hat, axis=-1, keepdims=True)
    second_part = normed * jnp.mean(grad_hat * normed, axis=-1, keepdims=True)
    return inverse * (grad_hat - first_part - second_part)


def dot(left, right, dims):
    return lax.dot_general(left, right, (((dims[0],), (dims[1],)), ((), ())), preferred_element_type=F32)


def attend(proj, gproj):
    scaling = HEAD ** (-0.5)
    for image in range(ROWS // IMG_TOK):
        at = pl.ds(image * IMG_TOK, IMG_TOK)
        query_hat, query_inverse = normalize(proj[at, :HEAD])
        key_hat, key_inverse = normalize(proj[at, HEAD : 2 * HEAD])
        query_low, key_low = query_hat.astype(BF16), key_hat.astype(BF16)
        value_low = proj[at, 2 * HEAD : 3 * HEAD].astype(BF16)
        grad_attended = proj[at, 3 * HEAD :].astype(BF16)
        exponent = jnp.exp(dot(query_low, key_low, (1, 1)) * scaling)
        attention = exponent / jnp.sum(exponent, axis=-1, keepdims=True)
        attention_low = attention.astype(BF16)
        gproj[at, 3 * HEAD :] = dot(attention_low, value_low, (1, 0)).astype(BF16)
        gproj[at, 2 * HEAD : 3 * HEAD] = dot(attention_low, grad_attended, (0, 0)).astype(BF16)
        grad_attention = dot(grad_attended, value_low, (1, 1))
        row_total = jnp.sum(attention * grad_attention, axis=-1, keepdims=True)
        grad_scores = (attention * (grad_attention - row_total) * scaling).astype(BF16)
        grad_query_hat = dot(grad_scores, key_low, (1, 0))
        grad_key_hat = dot(grad_scores, query_low, (0, 0))
        gproj[at, :HEAD] = norm_back(grad_query_hat, query_hat, query_inverse).astype(BF16)
        gproj[at, HEAD : 2 * HEAD] = norm_back(grad_key_hat, key_hat, key_inverse).astype(BF16)


def scatter(me, mail, tok, cot, gproj, acc, sib_out, sib_in, nout, nin, fsum, fout, fin_ab, fin_c, sems):
    bs, br, ns, nr, fs, fr = sems

    def terms(yh, c):
        at = [columns((yh * 4 + i) * 2 + c) for i in range(4)]
        inner = dot(turned[: 3 * HEAD], jnp.concatenate([tok[:, a] for a in at], 1), (1, 0))
        outer = dot(turned[3 * HEAD :], jnp.concatenate([cot[:, a] for a in at], 1), (1, 0))
        return jnp.concatenate([inner, outer], 0).T.reshape(2, 2, 4, 2, 48, 4 * HEAD)

    turned = gproj[...].T
    sib = []
    for yh in range(2):
        sib_out[yh] = terms(yh, 1 - me.c).astype(BF16)
        sib.append(mail.push(sib_out.at[yh], sib_in.at[yh], bs.at[yh], br.at[yh], me.sibling()))

    def combos(stage, p):
        order = ORDERS[p][::-1]
        axis, rest, gone = order[stage], order[stage + 1:], order[:stage]
        found = []
        for n in range(2 ** len(rest)):
            found.append({a: (n >> i) & 1 for i, a in enumerate(rest)} | {a: me.low[a] for a in gone})
        return axis, found

    base = (0, 4, 6)

    def near(stage, p, half):
        axis, found = combos(stage, p)
        for n, at in enumerate(found):
            yl, xl, zl = ((1 - me.low[a]) if a == axis else at[a] for a in "yxz")
            nout[p, half, base[stage] + n] = acc[half, yl, xl, :, zl, pl.ds(16 * p, 16), :].astype(BF16)
        where = (p, half, pl.ds(base[stage], len(found)))
        k = (stage * 3 + p) * 2 + half
        return mail.push(nout.at[where], nin.at[where], ns.at[k], nr.at[k], me.step(axis, 1 - 2 * half))

    def near_add(stage, p, half):
        axis, found = combos(stage, p)
        for n, at in enumerate(found):
            yl, xl, zl = (me.low[a] if a == axis else at[a] for a in "yxz")
            place = (half, yl, xl, slice(None), zl, pl.ds(16 * p, 16), slice(None))
            acc[place] = acc[place] + nin[p, half, base[stage] + n].astype(F32)

    flight = {}
    for yh in range(2):
        acc[yh] = terms(yh, me.c)
        sib[yh].wait_recv()
        acc[yh] = acc[yh] + sib_in[yh].astype(F32)
        for p in range(3):
            flight[p, yh] = near(0, p, yh)
    for stage in range(3):
        for half in range(2):
            for p in range(3):
                flight[p, half].wait_recv()
                near_add(stage, p, half)
                if stage < 2:
                    flight[p, half] = near(stage + 1, p, half)

    for yh in range(2):
        for zf in range(4):
            block = acc[yh, me.yl, me.xl, zf, me.zl]
            for xh in range(2):
                rows = block[24 * xh : 24 * xh + 24]
                rows = jnp.concatenate([rows[:, :256], rows[:, 256:]], 0)
                fsum[yh, zf, xh] = rows
                fout[yh, zf, xh] = rows.astype(BF16)
    early, late = [], []
    for k, f in enumerate(FAR_XY):
        yh, zf, xh, to = me.far(f)
        early.append(mail.push(fout.at[yh, :, xh, EARLY], fin_ab.at[k], fs.at[k], fr.at[k], to))
    for k, f in enumerate(FAR_Z):
        yh, zf, xh, to = me.far(f)
        late.append(mail.push(fout.at[:, zf, :, LATE], fin_c.at[k], fs.at[3 + k], fr.at[3 + k], to))
    for k in range(3):
        early[k].wait_recv()
        fsum[me.yh, :, me.xh, EARLY] += fin_ab[k].astype(F32)
    fout[me.yh, :, me.xh, EARLY] = fsum[me.yh, :, me.xh, EARLY].astype(BF16)
    copies = []
    for k, f in enumerate(FAR_Z):
        yh, zf, xh, to = me.far(f)
        copies.append(
            mail.push(fout.at[me.yh, zf, me.xh, EARLY], fin_ab.at[3, k], fs.at[6 + k], fr.at[6 + k], to)
        )
    for k in range(3):
        late[k].wait_recv()
        fsum[:, me.zf, :, LATE] += fin_c[k].astype(F32)
    fout[:, me.zf, :, LATE] = fsum[:, me.zf, :, LATE].astype(BF16)
    for k, f in enumerate(FAR_XY):
        yh, zf, xh, to = me.far(f)
        copies.append(
            mail.push(fout.at[yh, me.zf, xh, LATE], fin_c.at[3, k // 2, k % 2], fs.at[9 + k], fr.at[9 + k], to)
        )
    total_ab = fsum[me.yh, me.zf, me.xh, EARLY]
    total_c = fsum[me.yh, me.zf, me.xh, LATE]
    for k in range(3):
        copies[k].wait_recv()
        total_ab = total_ab + fin_ab[3, k].astype(F32)
    for k in range(3):
        copies[3 + k].wait_recv()
        total_c = total_c + fin_c[3, k // 2, k % 2].astype(F32)
    total = jnp.concatenate([total_ab, total_c], 0)
    return jnp.concatenate([total[:24], total[24:]], 1)


def adam_step(parameter, moment_one, moment_two, gradient, decay_rate):
    fresh_one = BETA_ONE * moment_one + (1.0 - BETA_ONE) * gradient
    fresh_two = BETA_TWO * moment_two + (1.0 - BETA_TWO) * gradient * gradient
    adjusted = fresh_one / CORRECT_ONE / (jnp.sqrt(fresh_two / CORRECT_TWO) + ADAM_EPS)
    return (parameter - LEARN_RATE * (adjusted + decay_rate * parameter), fresh_one, fresh_two)


def stacked(rows):
    return jnp.concatenate([rows[:, :256], rows[:, 256:]], 0).astype(BF16)


def gain_line(place, row):
    place[...] = jnp.zeros((1, 128), F32)
    place[:, :24] = row.astype(BF16).astype(F32)


def as_row(column):
    lane = lax.broadcasted_iota(jnp.int32, (24, 24), 1)
    row = lax.broadcasted_iota(jnp.int32, (24, 24), 0)
    return jnp.sum(jnp.where(lane == row, column, 0.0), axis=0, keepdims=True)


def whole(
    tokens, cotangent, weights, first, second, gain, gain_one, gain_two,
    new_weights, new_first, new_second, new_gain, new_gain_one, new_gain_two, next_weights, next_gain,
    tok, cot, full, full_two, gfull, gnext, land, land_two, shard, gains, mean, inverse, proj, gproj,
    acc, sib_out, sib_in, nout, nin, fsum, fout, fin_ab, fin_c, small, load, rsem, *sems
):
    me = Place()
    mail = Mail()
    loads = [pltpu.make_async_copy(tokens, tok, load.at[0]), pltpu.make_async_copy(cotangent, cot, load.at[1])]
    for copy in loads:
        copy.start()
    shard[...] = stacked(weights[...])
    gain_line(gfull.at[me.yh, me.yl, me.xl, me.c, me.zf, me.zl, me.xh], gain[...])
    enter(me)

    def far_one():
        loads[0].wait()
        statistics(tok, mean, inverse, 0, 16)

    def far_two():
        statistics(tok, mean, inverse, 16, 16)

    def gains_here(shared):
        shared.wait_recv()
        gains[...] = gain_rows(gfull)
        scale_tokens(tok, gains, mean, inverse, me.c)
        loads[1].wait()

    def own_here():
        scale_tokens(tok, gains, mean, inverse, 1 - me.c)
        project(tok, cot, full, proj, me.c, True)

    nothing = lambda: None
    gather(
        me, mail, shard, full, gfull, land, sems[:8],
        (far_one, far_two, nothing, nothing, nothing, gains_here, own_here),
    )
    project(tok, cot, full, proj, 1 - me.c, False)
    attend(proj, gproj)
    gradient = scatter(
        me, mail, tok, cot, gproj, acc, sib_out, sib_in, nout, nin, fsum, fout, fin_ab, fin_c, sems[16:]
    )
    low = weights[:, : 3 * HEAD].astype(BF16).astype(F32)
    grad_gain = as_row(jnp.sum(gradient[:, : 3 * HEAD] * low, axis=1, keepdims=True))
    grad_gain = grad_gain / gain[...].astype(BF16).astype(F32)
    fresh, one, two = adam_step(weights[...], first[...], second[...], gradient, DECAY_RATE)
    saves = []
    for k, (value, to) in enumerate(((fresh, new_weights), (one, new_first), (two, new_second))):
        small[k] = value
        saves.append(pltpu.make_async_copy(small.at[k], to, load.at[2 + k]))
        saves[-1].start()
    fresh_gain, one, two = adam_step(gain[...], gain_one[...], gain_two[...], grad_gain, 0.0)
    new_gain[...], new_gain_one[...], new_gain_two[...] = fresh_gain, one, two
    shard[...] = stacked(fresh)
    gain_line(gnext.at[me.yh, me.yl, me.xl, me.c, me.zf, me.zl, me.xh], fresh_gain)

    def next_here(shared):
        shared.wait_recv()
        next_gain[...] = gain_rows(gnext)

    gather(
        me, mail, shard, full_two, gnext, land_two, sems[8:16], (nothing,) * 5 + (next_here, nothing),
        next_weights, rsem,
    )
    for copy in saves:
        copy.wait()
    mail.close()


def keep(*refs):
    count = (len(refs) - 2) // 3
    here, there, held, came, left = refs[:count], refs[count : 2 * count], refs[2 * count : 3 * count], refs[-2], refs[-1]
    pairs = []
    for i in range(count):
        if len(here[i].shape) > 2:
            for n in range(8):
                at = (n // 4, n // 2 % 2, n % 2)
                pairs.append((here[i].at[at], held[i].at[at], there[i].at[at]))
        else:
            pairs.append((here[i], held[i], there[i]))
    ins = [pltpu.make_async_copy(a, b, came.at[k]) for k, (a, b, c) in enumerate(pairs)]
    outs = [pltpu.make_async_copy(b, c, left.at[k]) for k, (a, b, c) in enumerate(pairs)]
    for copy in ins:
        copy.start()
    for a, b in zip(ins, outs):
        a.wait()
        b.start()
    for copy in outs:
        copy.wait()


def shards(
    tokens, cotangent, weights, first_moment, second_moment, norm_gain, gain_first, gain_second
):
    dma, vmem = pltpu.SemaphoreType.DMA, pltpu.VMEM
    own, line = jax.ShapeDtypeStruct((24, 512), F32), jax.ShapeDtypeStruct((1, 24), F32)
    gather_sems = [dma((12,))] * 2 + [dma((9,))] * 2 + [dma((36,))] * 2 + [dma((14,))] * 2
    out = pl.pallas_call(
        whole,
        name="whole",
        out_shape=(own,) * 3 + (line,) * 3
        + (jax.ShapeDtypeStruct(VIEW, BF16), jax.ShapeDtypeStruct((16, CHUNK), F32)),
        in_specs=[pl.BlockSpec(memory_space=pl.ANY)] * 2 + [pl.BlockSpec(memory_space=pltpu.VMEM)] * 6,
        out_specs=(pl.BlockSpec(memory_space=pl.ANY),) * 3 + (pl.BlockSpec(memory_space=pltpu.VMEM),) * 3
        + (pl.BlockSpec(memory_space=pl.ANY), pl.BlockSpec(memory_space=pltpu.VMEM)),
        scratch_shapes=[
            vmem((ROWS, 6144), BF16),
            vmem((ROWS, 6144), BF16),
            vmem(VIEW, BF16),
            vmem(VIEW, BF16),
            vmem(GVIEW, F32),
            vmem(GVIEW, F32),
            vmem((2, 4, 2, 48, 256), BF16),
            vmem((2, 4, 2, 48, 256), BF16),
            vmem((48, 256), BF16),
            vmem((16, CHUNK), F32),
            vmem((ROWS, 1), F32),
            vmem((ROWS, 1), F32),
            vmem((ROWS, 4 * HEAD), F32),
            vmem((ROWS, 4 * HEAD), BF16),
            vmem((2, 2, 2, 4, 2, 48, 512), F32),
            vmem((2, 2, 2, 4, 2, 48, 512), BF16),
            vmem((2, 2, 2, 4, 2, 48, 512), BF16),
            vmem((3, 2, 7, 4, 16, 512), BF16),
            vmem((3, 2, 7, 4, 16, 512), BF16),
            vmem((2, 4, 2, 48, 256), F32),
            vmem((2, 4, 2, 48, 256), BF16),
            vmem((4, 4, 32, 256), BF16),
            vmem((4, 2, 2, 16, 256), BF16),
            vmem((3, 24, 512), F32),
            dma((5,)),
            dma((14,)),
        ] + gather_sems * 2 + [dma((2,))] * 2 + [dma((18,))] * 2 + [dma((12,))] * 2,
        compiler_params=pltpu.CompilerParams(
            collective_id=1, has_side_effects=True, vmem_limit_bytes=56 << 20
        ),
    )(
        tokens, cotangent, weights, first_moment, second_moment,
        norm_gain.reshape(1, 24), gain_first.reshape(1, 24), gain_second.reshape(1, 24),
    )
    kept = (0, 1, 2, 3, 4, 5, 6)
    copies = pl.pallas_call(
        keep,
        name="keep",
        out_shape=tuple(jax.ShapeDtypeStruct(out[i].shape, out[i].dtype) for i in kept),
        in_specs=[pl.BlockSpec(memory_space=pl.ANY)] * len(kept),
        out_specs=(pl.BlockSpec(memory_space=pl.ANY),) * len(kept),
        scratch_shapes=[vmem(out[i].shape, out[i].dtype) for i in kept] + [dma((len(kept) + 7,))] * 2,
        compiler_params=pltpu.CompilerParams(vmem_limit_bytes=16 << 20),
    )(*(out[i] for i in kept))
    return (
        *copies[:3],
        *(copy.reshape(24) for copy in copies[3:6]),
        copies[6].reshape(6144, 512),
        out[7].reshape(6144).astype(BF16),
    )


def solution(mesh):
    rows, line = P(("gx", "gy"), None), P(("gx", "gy"))
    return jax.shard_map(
        shards,
        mesh=mesh,
        in_specs=(rows,) * 5 + (line,) * 3,
        out_specs=(rows,) * 3 + (line,) * 3 + (P(), P()),
        check_vma=False,
    )
```

time: 711 us -> 130 us (0.18)
  waiting for transfers between devices: 336 us -> 0 us
  blocking collectives: 301 us -> 0 us
  Pallas kernels: 0 us -> 121 us
  matrix products: 29.3 us -> 0 us
  other arithmetic: 16.1 us -> 0.01 us
  between operations: 16 us -> 0.68 us
    reduce_scatter x2 -> x0, waiting for transfers between devices: 336 us -> none  [the longest x1 199 us: shards(): lax.psum_scatter(group_sums[0], 'gy', scatter_dimension=0, tiled=True)]
    unnamed x4 -> x0, blocking collectives: 155 us -> none
    all_gather x4 -> x0, blocking collectives: 146 us -> none  [the longest x1 42.3 us: shards(): lax.all_gather(low_weights, 'gy', axis=0, tiled=True)]
    pallas_call x0 -> x2, Pallas kernels: none -> 121 us  [the longest x1 117 us: shards(): pl.pallas_call(whole, name='whole', out_shape=(own,) * 3 + (line,) * 3 +...]
    dot_general x11 -> x0, matrix products: 29 us -> none  [the longest x1 7.31 us: local_terms(): jnp.dot(normed, low_weights[:, :3 * head_dim], preferred_element_type=jnp...]
  transfers between devices with their start and end apart: 4 -> 0, of which waited for: 2 -> 0; matrix products, arithmetic and copies ran while one was open for 2% -> 0% of each run, Pallas kernels for 0% -> 0%
where the time goes in v2:
time: 130 us; the launch traced here: 129 us
  Pallas kernels  121 us (93%)
  local copies, waits for them, and re-layouts  7.69 us (6%)
    pallas_call x1, Pallas kernels, shards(): pl.pallas_call(whole, name='whole', out_shape=(own,) * 3 + (line,) * 3 +...  117 us
    unnamed x16, local copies, waits for them, and re-layouts  7.08 us
    pallas_call x1, Pallas kernels, shards(): pl.pallas_call(keep, name='keep', out_shape=tuple((jax.ShapeDtypeStruct(o...  3.57 us

profile of v2, /device:TPU:1, one launch (start us, length us, event | category | flops | bytes accessed | tf_op | source)
XLA Modules:
  0.0 129.2 jit_solution(12484567859416563524)
XLA Ops:
  0.6 117.2 %whole.1 = (f32[24,512]{1,0:T(8,128)}, f32[24,512]{1,0:T(8,128)}, f32[24,512]{1,0:T(8,128)}, f32[1,24]{1,0:T(1,128)}, f32[1,24]{1,0:T(1,128)}, /*index=5*/f32[1,...) custom-call(bf16[512,6144]{1,0:T(8,128)(2,1)} %tokens.1, bf16[512,6144]{1,0:T(8,128)(2,1)} %cotangent.1, ...), custom_call_target="tpu_custom_call" | custom-call | tf_op jit(solution)/shard_map/whole/pallas_call | solution.py:506
  117.9 0.0 copy-start
  117.9 2.8 %copy-done = bf16[2,2,2,2,4,2,48,512]{7,6,5,4,3,2,1,0:T(8,128)(2,1)S(1)} copy-done((bf16[2,2,2,2,4,2,48,512]{7,6,5,4,3,2,1,0:T(8,128)(2,1)S(1)}, bf16[2,2,2,2,4,2,48,512]{7,6,5,4,3,2,1,0:T(8,128)(2,1)}, u32[]{:S(2)}) %copy-start) | copy-done | bytes 6291480
  120.7 0.0 copy-start.1
  120.7 0.8 copy-done.1
  121.5 0.0 copy-start.2
  121.5 0.8 copy-done.2
  122.3 0.0 copy-start.3
  122.3 0.8 copy-done.3
  123.1 0.0 copy-start.4
  123.1 0.6 copy-done.4
  123.7 0.0 copy-start.5
  123.7 0.6 copy-done.5
  124.3 0.0 copy-start.6
  124.3 0.7 copy-done.6
  125.0 0.0 copy-start.7
  125.0 3.6 %keep.1 = (f32[24,512]{1,0:T(8,128)}, f32[24,512]{1,0:T(8,128)}, f32[24,512]{1,0:T(8,128)}, f32[1,24]{1,0:T(1,128)}, f32[1,24]{1,0:T(1,128)}, /*index=5*/f32[1,2...) custom-call(f32[24,512]{1,0:T(8,128)S(1)} %copy-done.1, f32[24,512]{1,0:T(8,128)S(1)} %copy-done.2, ...), custom_call_target="tpu_custom_call" | custom-call | tf_op jit(solution)/shard_map/keep/pallas_call | solution.py:550
  128.5 0.0 copy-done.7
  128.6 0.6 convert_element_type.7
  (1 shorter events, 0.0 us)
Async XLA Ops:
  117.9 2.8 %copy-start = (bf16[2,2,2,2,4,2,48,512]{7,6,5,4,3,2,1,0:T(8,128)(2,1)S(1)}, bf16[2,2,2,2,4,2,48,512]{7,6,5,4,3,2,1,0:T(8,128)(2,1)}, u32[]{:S(2)}) copy-start(bf16[2,2,2,2,4,2,48,512]{7,6,5,4,3,2,1,0:T(8,128)(2,1)} %get-tuple-element.29.refs_6_) | copy-start | bytes 18874372
  120.7 0.8 copy-start.1
  121.5 0.8 copy-start.2
  122.3 0.8 copy-start.3
  123.1 0.6 copy-start.4
  123.7 0.6 copy-start.5
  124.3 0.7 copy-start.6
  125.0 3.6 %copy-start.7 = (f32[16,384]{1,0:T(8,128)S(1)}, f32[16,384]{1,0:T(8,128)}, u32[]{:S(2)}) copy-start(f32[16,384]{1,0:T(8,128)} %get-tuple-element.37) | copy-start | bytes 73732

commit v3 on v2

--- a/solution.py
+++ b/solution.py
@@ -182,7 +182,7 @@
             for half in range(2):
                 flight[2, p, half, q].wait_recv()
         spread_news(2, pl.ds(2 * q, 2))
-    between[6]()
+        between[6 + q]()
     for k, copy in enumerate(shared):
         if k != 7:
             copy.wait_recv()
@@ -307,21 +307,23 @@
 
     base = (0, 4, 6)
 
-    def near(stage, p, half):
+    def near(stage, p, yh, way):
         axis, found = combos(stage, p)
+        zfar = pl.ds(2 * way, 2)
         for n, at in enumerate(found):
             yl, xl, zl = ((1 - me.low[a]) if a == axis else at[a] for a in "yxz")
-            nout[p, half, base[stage] + n] = acc[half, yl, xl, :, zl, pl.ds(16 * p, 16), :].astype(BF16)
-        where = (p, half, pl.ds(base[stage], len(found)))
-        k = (stage * 3 + p) * 2 + half
-        return mail.push(nout.at[where], nin.at[where], ns.at[k], nr.at[k], me.step(axis, 1 - 2 * half))
-
-    def near_add(stage, p, half):
+            nout[p, yh, base[stage] + n, zfar] = acc[yh, yl, xl, zfar, zl, pl.ds(16 * p, 16), :].astype(BF16)
+        where = (p, yh, pl.ds(base[stage], len(found)), zfar)
+        k = ((stage * 3 + p) * 2 + yh) * 2 + way
+        return mail.push(nout.at[where], nin.at[where], ns.at[k], nr.at[k], me.step(axis, 1 - 2 * way))
+
+    def near_add(stage, p, yh, way):
         axis, found = combos(stage, p)
+        zfar = pl.ds(2 * way, 2)
         for n, at in enumerate(found):
             yl, xl, zl = (me.low[a] if a == axis else at[a] for a in "yxz")
-            place = (half, yl, xl, slice(None), zl, pl.ds(16 * p, 16), slice(None))
-            acc[place] = acc[place] + nin[p, half, base[stage] + n].astype(F32)
+            place = (yh, yl, xl, zfar, zl, pl.ds(16 * p, 16), slice(None))
+            acc[place] = acc[place] + nin[p, yh, base[stage] + n, zfar].astype(F32)
 
     flight = {}
     for yh in range(2):
@@ -329,14 +331,16 @@
         sib[yh].wait_recv()
         acc[yh] = acc[yh] + sib_in[yh].astype(F32)
         for p in range(3):
-            flight[p, yh] = near(0, p, yh)
+            for way in range(2):
+                flight[p, yh, way] = near(0, p, yh, way)
     for stage in range(3):
-        for half in range(2):
+        for yh in range(2):
             for p in range(3):
-                flight[p, half].wait_recv()
-                near_add(stage, p, half)
-                if stage < 2:
-                    flight[p, half] = near(stage + 1, p, half)
+                for way in range(2):
+                    flight[p, yh, way].wait_recv()
+                    near_add(stage, p, yh, way)
+                    if stage < 2:
+                        flight[p, yh, way] = near(stage + 1, p, yh, way)
 
     for yh in range(2):
         for zf in range(4):
@@ -423,10 +427,13 @@
 
     def far_one():
         loads[0].wait()
-        statistics(tok, mean, inverse, 0, 16)
+        statistics(tok, mean, inverse, 0, 14)
 
     def far_two():
-        statistics(tok, mean, inverse, 16, 16)
+        statistics(tok, mean, inverse, 14, 10)
+
+    def near_one():
+        statistics(tok, mean, inverse, 24, 8)
 
     def gains_here(shared):
         shared.wait_recv()
@@ -434,14 +441,16 @@
         scale_tokens(tok, gains, mean, inverse, me.c)
         loads[1].wait()
 
+    def scale_here():
+        scale_tokens(tok, gains, mean, inverse, 1 - me.c)
+
     def own_here():
-        scale_tokens(tok, gains, mean, inverse, 1 - me.c)
         project(tok, cot, full, proj, me.c, True)
 
     nothing = lambda: None
     gather(
         me, mail, shard, full, gfull, land, sems[:8],
-        (far_one, far_two, nothing, nothing, nothing, gains_here, own_here),
+        (far_one, far_two, near_one, nothing, nothing, gains_here, scale_here, own_here),
     )
     project(tok, cot, full, proj, 1 - me.c, False)
     attend(proj, gproj)
@@ -467,7 +476,7 @@
         next_gain[...] = gain_rows(gnext)
 
     gather(
-        me, mail, shard, full_two, gnext, land_two, sems[8:16], (nothing,) * 5 + (next_here, nothing),
+        me, mail, shard, full_two, gnext, land_two, sems[8:16], (nothing,) * 5 + (next_here, nothing, nothing),
         next_weights, rsem,
     )
     for copy in saves:
@@ -538,7 +547,7 @@
             vmem((3, 24, 512), F32),
             dma((5,)),
             dma((14,)),
-        ] + gather_sems * 2 + [dma((2,))] * 2 + [dma((18,))] * 2 + [dma((12,))] * 2,
+        ] + gather_sems * 2 + [dma((2,))] * 2 + [dma((36,))] * 2 + [dma((12,))] * 2,
         compiler_params=pltpu.CompilerParams(
             collective_id=1, has_side_effects=True, vmem_limit_bytes=56 << 20
         ),
@@ -551,7 +560,7 @@
         keep,
         name="keep",
         out_shape=tuple(jax.ShapeDtypeStruct(out[i].shape, out[i].dtype) for i in kept),
-        in_specs=[pl.BlockSpec(memory_space=pl.ANY)] * len(kept),
+        in_specs=[pl.BlockSpec(memory_space=pltpu.HBM)] * len(kept),
         out_specs=(pl.BlockSpec(memory_space=pl.ANY),) * len(kept),
         scratch_shapes=[vmem(out[i].shape, out[i].dtype) for i in kept] + [dma((len(kept) + 7,))] * 2,
         compiler_params=pltpu.CompilerParams(vmem_limit_bytes=16 << 20),

time: 130 us -> 126 us (0.969)
  Pallas kernels: 121 us -> 117 us
    pallas_call x1, Pallas kernels: 117 us -> 114 us  [shards(): pl.pallas_call(whole, name='whole', out_shape=(own,) * 3 + (line,) * 3 +...]
where the time goes in v3:
time: 126 us
  Pallas kernels  117 us (93%)
  local copies, waits for them, and re-layouts  7.69 us (6%)
    pallas_call x1, Pallas kernels, shards(): pl.pallas_call(whole, name='whole', out_shape=(own,) * 3 + (line,) * 3 +...  114 us
    unnamed x16, local copies, waits for them, and re-layouts  7.08 us
    pallas_call x1, Pallas kernels, shards(): pl.pallas_call(keep, name='keep', out_shape=tuple((jax.ShapeDtypeStruct(o...  3.57 us

profile of v3, /device:TPU:1, one launch (start us, length us, event | category | flops | bytes accessed | tf_op | source)
XLA Modules:
  0.0 125.6 jit_solution(13787818947788429434)
XLA Ops:
  0.6 113.7 %whole.1 = (f32[24,512]{1,0:T(8,128)}, f32[24,512]{1,0:T(8,128)}, f32[24,512]{1,0:T(8,128)}, f32[1,24]{1,0:T(1,128)}, f32[1,24]{1,0:T(1,128)}, /*index=5*/f32[1,...) custom-call(bf16[512,6144]{1,0:T(8,128)(2,1)} %tokens.1, bf16[512,6144]{1,0:T(8,128)(2,1)} %cotangent.1, ...), custom_call_target="tpu_custom_call" | custom-call | tf_op jit(solution)/shard_map/whole/pallas_call | solution.py:515
  114.3 0.0 copy-start
  114.3 2.8 %copy-done = bf16[2,2,2,2,4,2,48,512]{7,6,5,4,3,2,1,0:T(8,128)(2,1)S(1)} copy-done((bf16[2,2,2,2,4,2,48,512]{7,6,5,4,3,2,1,0:T(8,128)(2,1)S(1)}, bf16[2,2,2,2,4,2,48,512]{7,6,5,4,3,2,1,0:T(8,128)(2,1)}, u32[]{:S(2)}) %copy-start) | copy-done | bytes 6291480
  117.1 0.0 copy-start.1
  117.1 0.8 copy-done.1
  117.9 0.0 copy-start.2
  117.9 0.8 copy-done.2
  118.7 0.0 copy-start.3
  118.7 0.8 copy-done.3
  119.5 0.0 copy-start.4
  119.5 0.6 copy-done.4
  120.1 0.0 copy-start.5
  120.1 0.6 copy-done.5
  120.7 0.0 copy-start.6
  120.7 0.7 copy-done.6
  121.4 0.0 copy-start.7
  121.4 3.6 %keep.1 = (f32[24,512]{1,0:T(8,128)}, f32[24,512]{1,0:T(8,128)}, f32[24,512]{1,0:T(8,128)}, f32[1,24]{1,0:T(1,128)}, f32[1,24]{1,0:T(1,128)}, /*index=5*/f32[1,2...) custom-call(f32[24,512]{1,0:T(8,128)S(1)} %copy-done.1, f32[24,512]{1,0:T(8,128)S(1)} %copy-done.2, ...), custom_call_target="tpu_custom_call" | custom-call | tf_op jit(solution)/shard_map/keep/pallas_call | solution.py:559
  125.0 0.0 copy-done.7
  125.0 0.6 convert_element_type.7
  (1 shorter events, 0.0 us)
Async XLA Ops:
  114.3 2.8 %copy-start = (bf16[2,2,2,2,4,2,48,512]{7,6,5,4,3,2,1,0:T(8,128)(2,1)S(1)}, bf16[2,2,2,2,4,2,48,512]{7,6,5,4,3,2,1,0:T(8,128)(2,1)}, u32[]{:S(2)}) copy-start(bf16[2,2,2,2,4,2,48,512]{7,6,5,4,3,2,1,0:T(8,128)(2,1)} %get-tuple-element.29.refs_6_) | copy-start | bytes 18874372
  117.1 0.8 copy-start.1
  117.9 0.8 copy-start.2
  118.7 0.8 copy-start.3
  119.5 0.6 copy-start.4
  120.1 0.6 copy-start.5
  120.7 0.7 copy-start.6
  121.4 3.6 %copy-start.7 = (f32[16,384]{1,0:T(8,128)S(1)}, f32[16,384]{1,0:T(8,128)}, u32[]{:S(2)}) copy-start(f32[16,384]{1,0:T(8,128)} %get-tuple-element.37) | copy-start | bytes 73732

commit v4 on v3

--- a/solution.py
+++ b/solution.py
@@ -560,10 +560,10 @@
         keep,
         name="keep",
         out_shape=tuple(jax.ShapeDtypeStruct(out[i].shape, out[i].dtype) for i in kept),
-        in_specs=[pl.BlockSpec(memory_space=pltpu.HBM)] * len(kept),
+        in_specs=[pl.BlockSpec(memory_space=pl.ANY)] * len(kept),
         out_specs=(pl.BlockSpec(memory_space=pl.ANY),) * len(kept),
         scratch_shapes=[vmem(out[i].shape, out[i].dtype) for i in kept] + [dma((len(kept) + 7,))] * 2,
-        compiler_params=pltpu.CompilerParams(vmem_limit_bytes=16 << 20),
+        compiler_params=pltpu.CompilerParams(vmem_limit_bytes=60 << 20),
     )(*(out[i] for i in kept))
     return (
         *copies[:3],

time: 126 us -> 121 us (0.960)
  local copies, waits for them, and re-layouts: 7.69 us -> 0.62 us
  Pallas kernels: 117 us -> 119 us
    unnamed x16 -> x2, local copies, waits for them, and re-layouts: 7.08 us -> 0.01 us
    pallas_call x1, Pallas kernels: 3.57 us -> 5.77 us  [shards(): pl.pallas_call(keep, name='keep', out_shape=tuple((jax.ShapeDtypeStruct(o...]
where the time goes in v4:
time: 121 us
  Pallas kernels  119 us (98%)
    pallas_call x1, Pallas kernels, shards(): pl.pallas_call(whole, name='whole', out_shape=(own,) * 3 + (line,) * 3 +...  114 us
    pallas_call x1, Pallas kernels, shards(): pl.pallas_call(keep, name='keep', out_shape=tuple((jax.ShapeDtypeStruct(o...  5.77 us

profile of v4, /device:TPU:1, one launch (start us, length us, event | category | flops | bytes accessed | tf_op | source)
XLA Modules:
  0.0 120.7 jit_solution(16410033592234778193)
XLA Ops:
  0.6 113.7 %whole.1 = (f32[24,512]{1,0:T(8,128)}, f32[24,512]{1,0:T(8,128)}, f32[24,512]{1,0:T(8,128)}, f32[1,24]{1,0:T(1,128)}, f32[1,24]{1,0:T(1,128)}, /*index=5*/f32[1,...) custom-call(bf16[512,6144]{1,0:T(8,128)(2,1)} %tokens.1, bf16[512,6144]{1,0:T(8,128)(2,1)} %cotangent.1, ...), custom_call_target="tpu_custom_call" | custom-call | tf_op jit(solution)/shard_map/whole/pallas_call | solution.py:515
  114.3 0.0 copy-start
  114.3 5.8 %keep.1 = (f32[24,512]{1,0:T(8,128)}, f32[24,512]{1,0:T(8,128)}, f32[24,512]{1,0:T(8,128)}, f32[1,24]{1,0:T(1,128)}, f32[1,24]{1,0:T(1,128)}, /*index=5*/f32[1,2...) custom-call(f32[24,512]{1,0:T(8,128)} %get-tuple-element.23.refs_0_, f32[24,512]{1,0:T(8,128)} %get-tuple-element.24.refs_1_, ...), custom_call_target="tpu_custom_call" | custom-call | tf_op jit(solution)/shard_map/keep/pallas_call | solution.py:559
  120.1 0.0 copy-done
  120.1 0.6 convert_element_type.7
  (1 shorter events, 0.0 us)
Async XLA Ops:
  114.3 5.8 %copy-start = (f32[16,384]{1,0:T(8,128)S(1)}, f32[16,384]{1,0:T(8,128)}, u32[]{:S(2)}) copy-start(f32[16,384]{1,0:T(8,128)} %get-tuple-element.37) | copy-start | bytes 73732

commit v5 on v4

--- a/solution.py
+++ b/solution.py
@@ -158,8 +158,8 @@
                 k = ((stage * 3 + p) * 2 + half) * 2 + q
                 flight[stage, p, half, q] = mail.push(src, src, ns.at[k], nr.at[k], me.step(axis, 1 - 2 * half))
 
-    def spread_news(stage, zfar):
-        for p in range(3):
+    def spread_news(stage, zfar, parts=(0, 1, 2)):
+        for p in parts:
             share(lambda ref: part(ref, ORDERS[p][:stage], both, zfar, p, ORDERS[p][stage]), full)
 
     near(0, 0)
@@ -181,7 +181,7 @@
         for p in range(3):
             for half in range(2):
                 flight[2, p, half, q].wait_recv()
-        spread_news(2, pl.ds(2 * q, 2))
+            spread_news(2, pl.ds(2 * q, 2), (p,))
         between[6 + q]()
     for k, copy in enumerate(shared):
         if k != 7:

time: 121 us -> 120 us (level)
  no operation moved by 1% of the time
where the time goes in v5:
time: 120 us
  Pallas kernels  119 us (99%)
    pallas_call x1, Pallas kernels, shards(): pl.pallas_call(whole, name='whole', out_shape=(own,) * 3 + (line,) * 3 +...  113 us
    pallas_call x1, Pallas kernels, shards(): pl.pallas_call(keep, name='keep', out_shape=tuple((jax.ShapeDtypeStruct(o...  5.77 us

profile of v5, /device:TPU:1, one launch (start us, length us, event | category | flops | bytes accessed | tf_op | source)
XLA Modules:
  0.0 120.3 jit_solution(7947876496522754542)
XLA Ops:
  0.6 113.2 %whole.1 = (f32[24,512]{1,0:T(8,128)}, f32[24,512]{1,0:T(8,128)}, f32[24,512]{1,0:T(8,128)}, f32[1,24]{1,0:T(1,128)}, f32[1,24]{1,0:T(1,128)}, /*index=5*/f32[1,...) custom-call(bf16[512,6144]{1,0:T(8,128)(2,1)} %tokens.1, bf16[512,6144]{1,0:T(8,128)(2,1)} %cotangent.1, ...), custom_call_target="tpu_custom_call" | custom-call | tf_op jit(solution)/shard_map/whole/pallas_call | solution.py:515
  113.8 0.0 copy-start
  113.9 5.8 %keep.1 = (f32[24,512]{1,0:T(8,128)}, f32[24,512]{1,0:T(8,128)}, f32[24,512]{1,0:T(8,128)}, f32[1,24]{1,0:T(1,128)}, f32[1,24]{1,0:T(1,128)}, /*index=5*/f32[1,2...) custom-call(f32[24,512]{1,0:T(8,128)} %get-tuple-element.23.refs_0_, f32[24,512]{1,0:T(8,128)} %get-tuple-element.24.refs_1_, ...), custom_call_target="tpu_custom_call" | custom-call | tf_op jit(solution)/shard_map/keep/pallas_call | solution.py:559
  119.6 0.0 copy-done
  119.7 0.6 convert_element_type.7
  (1 shorter events, 0.0 us)
Async XLA Ops:
  113.8 5.8 %copy-start = (f32[16,384]{1,0:T(8,128)S(1)}, f32[16,384]{1,0:T(8,128)}, u32[]{:S(2)}) copy-start(f32[16,384]{1,0:T(8,128)} %get-tuple-element.37) | copy-start | bytes 73732
